TPU v7x, 32 devices: a whole 2x2x4 slice. The times are simulated.
32 devices in a mesh: groups: 2 (over y), rows: 8 (over z, x), member: 2 (over core).
Axes of the slice: x: 2, y: 2, z: 4, core: 2. Of those that a mesh axis runs over, the one named last changes fastest.
Arguments:
- features: bfloat16 [16384, 512], P(('groups', 'rows')), parts along dimension 0, may hold values from -6 to 6
- escalated: int32 [16, 256], P(('groups', 'rows')), parts along dimension 0, may hold values from 0 to 1023, as said below
- owner_ids: int32 [16, 256, 1], P(('groups', 'rows')), parts along dimension 0, may hold values from 0 to 7; in each aligned block of 256 rows (0 to 255, 256 to 511, ..., all dimensions but the last counted through in order) at most 64 rows name the same one
- member_in: bfloat16 [4, 512, 1024], P('member'), may hold values from -0.25 to 0.25
- member_bias: float32 [4, 1024], P('member'), may hold values from -3 to 3
- member_out: bfloat16 [4, 1024], P('member'), may hold values from -0.1875 to 0.1875
- feat_weight: bfloat16 [512, 512], P('member'), may hold values from -0.25 to 0.25
- feat_bias: float32 [512], replicated, may hold values from -5 to 5
- pred_scale: float32 [4, 512], replicated, may hold values from -5 to 5
- pred_shift: float32 [4, 512], replicated, may hold values from -5 to 5
- cls_token: float32 [512], replicated, may hold values from -5 to 5
- attn_gain: float32 [512], replicated, may hold values from 0.1 to 1.9
- qkv_weight: bfloat16 [3, 512, 512], P(None, None, 'member'), may hold values from -0.25 to 0.25
- out_weight: bfloat16 [512, 512], P('member'), may hold values from -0.25 to 0.25
- ffn_gain: float32 [512], replicated, may hold values from 0.1 to 1.9
- up_weight: bfloat16 [8, 512, 1024], P('rows', None, 'member'), may hold values from -0.25 to 0.25
- up_bias: float32 [8, 1024], P('rows', 'member'), may hold values from -3 to 3
- down_weight: bfloat16 [8, 1024, 512], P('rows', 'member'), may hold values from -0.1875 to 0.1875
- owner_heads: float32 [8, 512], P('rows'), may hold values from -0.25 to 0.25
Outputs:
- scores: float32 [16384], P(('groups', 'rows')), parts along dimension 0
There are 2 independent parts, one for each index of `groups`. A program takes and returns all parts, laid end to end along the dimension named above; an argument that names none is the same for every part. Nothing has to cross between parts.
Inputs may be any that keep to these rules, and one draw needn't show every extreme that they name: Each row of escalated lists 256 distinct local row indices of its shard. `owner_ids`: within one row shard at most 64 escalated rows have the same segment.
All inputs are finite; a program needn't handle non-finite values.
Results may differ from a plain program's by a relative error of at most 0.0034.
Values may be sent and summed in bfloat16 or wider, within the bound.
No kernel may reach another device: no remote copies, remote signals or barrier semaphores. Data moves between devices by JAX's collectives and lax.ppermute only.
A program may use at most 64 MiB of HBM per device.

v0:
```python
import functools
import math

import jax
import jax.numpy as jnp
from jax import lax
from jax.experimental import pallas as pl
from jax.experimental.pallas import tpu as pltpu
from jax.sharding import PartitionSpec as P

HD = 64
EPS = 1e-05
LANES = 128
BF = jnp.bfloat16
F32 = jnp.float32
VMEM = pl.BlockSpec(memory_space=pltpu.VMEM)
HBM = pl.BlockSpec(memory_space=pltpu.HBM)
ANY = pl.BlockSpec(memory_space=pl.ANY)
GELU_C = math.sqrt(2.0 / math.pi)

KMAP, VCLS, LCLS, SCALE, SHIFT, GAIN, FBIAS, CLS, FGAIN = 0, 8, 9, 16, 24, 32, 33, 34, 35
TABLE = 40
DOWN, BIAS, HEAD, EXTRA = 0, 3, 6, 16


def iota(shape, dim):
    return lax.broadcasted_iota(jnp.int32, shape, dim)


def gelu2(x):
    return x + x * jnp.tanh(x * (GELU_C + (GELU_C * 0.044715) * (x * x)))


def dot(a, b):
    return lax.dot_general(a, b, (((1,), (0,)), ((), ())), preferred_element_type=F32)


def dot_t(a, b):
    return lax.dot_general(a, b, (((1,), (1,)), ((), ())), preferred_element_type=F32)


def split2(x):
    high = x.astype(BF)
    return high, (x - high.astype(F32)).astype(BF)


def split3(x):
    high, rest = x.astype(BF), x
    rest = rest - high.astype(F32)
    mid = rest.astype(BF)
    low = (rest - mid.astype(F32)).astype(BF)
    return jnp.concatenate([high.astype(F32), mid.astype(F32), low.astype(F32)], axis=0).astype(BF)


def join3(x):
    rows = x.shape[0] // 3
    return x[:rows] + x[rows : 2 * rows] + x[2 * rows :]


def centre(x):
    return x - jnp.mean(x, axis=-1, keepdims=True)


def inverse_spread(centered):
    return lax.rsqrt(jnp.mean(centered * centered, axis=-1, keepdims=True) + EPS)


def start_all(pairs, sems):
    copies = [pltpu.make_async_copy(src, dst, sems.at[i]) for i, (src, dst) in enumerate(pairs)]
    for copy in copies:
        copy.start()
    return copies


def route_kernel(
    n, half, relative, esc_hbm, own_hbm, feat_hbm, down_hbm, up_hbm, fw_hbm, ow_hbm,
    index_ref, rows_ref, down_ref, segment_ref, both_ref, esc_ref, own_ref, feat_ref, sems,
):
    copies = start_all(
        [(esc_hbm, esc_ref), (own_hbm, own_ref), (feat_hbm, feat_ref), (down_hbm.at[0], down_ref),
         (fw_hbm, both_ref.at[: fw_hbm.shape[0]]), (ow_hbm, both_ref.at[fw_hbm.shape[0] :]),
         (up_hbm.at[0], segment_ref.at[: up_hbm.shape[1]])], sems)
    segment_ref[up_hbm.shape[1] :, :] = jnp.zeros((EXTRA, up_hbm.shape[2]), BF)
    core = lax.axis_index("member")
    count = esc_hbm.shape[1]
    dealt = count // 2
    copies[0].wait()
    copies[1].wait()
    esc = esc_ref[...]
    own = own_ref[...]
    ii = iota((count, count), 0)
    jj = iota((count, count), 1)
    own_col = jnp.sum(jnp.where(ii == jj, own, 0).astype(F32), axis=1, keepdims=True).astype(jnp.int32)
    before = jnp.sum((own_col < own).astype(F32), axis=0, keepdims=True).astype(jnp.int32)
    rank = jnp.sum(((own_col == own) & (ii < jj)).astype(F32), axis=0, keepdims=True).astype(jnp.int32)
    position = before + rank
    side = position & 1
    slot = rank >> 1
    apart = own ^ lax.axis_index("rows")
    pair = apart if relative else (own - (own & 1)) + (apart & 1)
    place = pair * half + slot
    dense = (position >> 1) + jnp.where(side == core, 0, dealt)
    source = jnp.sum(jnp.where(dense == ii, esc, 0).astype(F32), axis=1, keepdims=True).astype(jnp.int32)
    chosen = (source == iota((count, feat_ref.shape[0]), 1)).astype(F32).astype(BF)
    line = pair >> 1
    line = line * (n // 2 + 1) + (side ^ core) * (n // 2) ** 2 if relative else line + (side ^ core) * (n // 2)
    for i, row in enumerate((line, (apart & 1) * half + slot, esc, place, dense)):
        index_ref[i : i + 1, :] = row
    copies[2].wait()
    rows_ref[...] = dot(chosen, feat_ref[...]).astype(BF)
    for copy in copies[3:]:
        copy.wait()


def predict_kernel(
    rows_ref, w_ref, bias_ref, out_ref, upb_ref, head_ref, down_ref, raw_ref,
    near_ref, far_ref, segment_ref,
):
    depth = raw_ref.shape[0] - EXTRA
    here = w_ref.shape[0]
    core = lax.axis_index("member")
    dealt = near_ref.shape[0]
    lane = iota((8, 1), 0)
    preds = None
    for m in range(here):
        act = gelu2(dot(rows_ref[...], w_ref[m]) + bias_ref[m : m + 1]).astype(BF)
        on_lane = jnp.where(lane == core * here + m, 0.5 * out_ref[m : m + 1].astype(F32), 0.0).astype(BF)
        pred = dot_t(act, on_lane)
        preds = pred if preds is None else preds + pred
    preds = preds.astype(BF)
    near_ref[...] = preds[:dealt]
    far_ref[...] = preds[dealt:]
    head = split3(head_ref[...]).astype(F32)
    head = jnp.concatenate([head, jnp.zeros((LANES - 3, head.shape[1]), F32)], axis=0).astype(BF)
    down = jnp.sum(dot_t(down_ref[...], head).T[:8], axis=0, keepdims=True)
    extra = [split3(x).astype(F32) for x in (down, upb_ref[...], head_ref[...])]
    extra.append(jnp.zeros((EXTRA - 9, down.shape[1]), F32))
    segment_ref[depth:, :] = jnp.concatenate(extra, axis=0).astype(BF)


def constants_kernel(
    cls_ref, gain_ref, scale_ref, shift_ref, fbias_ref, fgain_ref, q0_ref, q1_ref, index_ref,
    table_ref, where_ref, place_ref,
):
    count = index_ref.shape[1]
    diag = iota((count, count), 0) == iota((count, count), 1)
    cols = [
        jnp.sum(jnp.where(diag, index_ref[i : i + 1, :], 0).astype(F32), axis=1, keepdims=True) for i in range(5)]
    for i in range(3):
        where_ref[:, i : i + 1] = cols[i].astype(jnp.int32)
    dealt = place_ref.shape[1]
    placed = cols[4].astype(jnp.int32) == iota((count, dealt), 1)
    place_ref[...] = jnp.sum(jnp.where(placed, cols[3], 0.0), axis=0, keepdims=True).astype(jnp.int32)
    gain = gain_ref[...]
    cls = cls_ref[...]
    centered = centre(cls)
    ncls = (centered * inverse_spread(centered) * gain).astype(BF)
    table_ref[...] = jnp.zeros_like(table_ref)
    members = scale_ref.shape[0]
    table_ref[SCALE : SCALE + members, :] = centre(scale_ref[...])
    table_ref[SHIFT : SHIFT + members, :] = centre(shift_ref[...])
    table_ref[GAIN : GAIN + 1, :] = gain
    table_ref[FBIAS : FBIAS + 1, :] = fbias_ref[...]
    table_ref[CLS : CLS + 1, :] = cls
    table_ref[FGAIN : FGAIN + 1, :] = fgain_ref[...]
    lhs = jnp.broadcast_to(ncls.astype(F32), (8, ncls.shape[1])).astype(BF)
    local = q0_ref.shape[2]
    heads = local // HD
    row = iota((8, local), 0)
    col = iota((8, local), 1) // HD
    kmap = None
    for i, ref in enumerate((q0_ref, q1_ref)):
        query = dot(lhs, ref[0]) * (1.0 / math.sqrt(HD))
        spread = jnp.where(row == col + i * heads, query, 0.0)
        part = join3(dot_t(split3(spread), ref[1]))
        kmap = part if kmap is None else kmap + part
        table_ref[VCLS : VCLS + 1, i * local : (i + 1) * local] = dot(lhs, ref[2])[0:1]
    table_ref[KMAP : KMAP + 8, :] = kmap
    logits = jnp.sum(kmap * ncls.astype(F32), axis=-1, keepdims=True)
    eye = iota((8, LANES), 0) == iota((8, LANES), 1)
    table_ref[LCLS : LCLS + 1, :LANES] = jnp.sum(jnp.where(eye, logits, 0.0), axis=0, keepdims=True)


def attend_kernel(
    members, rows_ref, near_ref, far_ref, place_ref, table_ref, fw0_ref, fw1_ref, q0_ref, q1_ref, *sent_refs
):
    core = lax.axis_index("member")
    total = near_ref.shape[0]
    fwidth = rows_ref.shape[1]
    rows = rows_ref[:total]
    local = q0_ref.shape[2]
    gain = table_ref[GAIN : GAIN + 1, :]
    low, high = rows[:, : fwidth // 2].astype(F32), rows[:, fwidth // 2 :].astype(F32)
    first = jnp.where(core == 0, low, high).astype(BF)
    second = jnp.where(core == 0, high, low).astype(BF)
    token = dot(first, fw0_ref[: fwidth // 2]) + dot(second, fw1_ref[: fwidth // 2]) + table_ref[FBIAS : FBIAS + 1, :]
    centered = centre(token)
    tokens = [(centered * inverse_spread(centered) * gain).astype(BF)]
    preds = near_ref[...].astype(F32) + far_ref[...].astype(F32)
    for m in range(members):
        centered = preds[:, m : m + 1] * table_ref[SCALE + m : SCALE + m + 1, :] + table_ref[SHIFT + m : SHIFT + m + 1, :]
        tokens.append((centered * inverse_spread(centered) * gain).astype(BF))
    normed = jnp.concatenate(tokens, axis=0)
    count = len(tokens)

    kmap = jnp.concatenate([table_ref[KMAP : KMAP + 8, :], jnp.zeros((LANES - 8, table_ref.shape[1]), F32)], axis=0)
    logits = dot_t(normed, jnp.concatenate(split2(kmap), axis=0))
    logits = logits[:, :LANES] + logits[:, LANES:]
    expo = jnp.exp(logits)
    expo_cls = jnp.exp(table_ref[LCLS : LCLS + 1, :LANES])
    norm = expo_cls
    for t in range(count):
        norm = norm + expo[t * total : (t + 1) * total]
    inverse = 1.0 / norm
    weights = jnp.concatenate(
        [expo[t * total : (t + 1) * total] * inverse for t in range(count)] + [expo_cls * inverse], axis=0)
    expand = (iota((2 * LANES, 2 * local), 0) & (LANES - 1)) == iota((2 * LANES, 2 * local), 1) // HD
    spread = dot(jnp.concatenate(split2(weights), axis=1), expand.astype(F32).astype(BF))
    parts = []
    for i, ref in enumerate((q0_ref, q1_ref)):
        at = slice(i * local, (i + 1) * local)
        value = dot(normed, ref[2])
        mixed = spread[count * total :, at] * table_ref[VCLS : VCLS + 1, at]
        for t in range(count):
            rng = slice(t * total, (t + 1) * total)
            mixed = mixed + spread[rng, at] * value[rng]
        parts.append(mixed)
    mixed = jnp.concatenate(parts, axis=1).astype(BF)
    size = sent_refs[0].shape[0]
    scatter = (place_ref[...] == iota((size * len(sent_refs), total), 0)).astype(F32).astype(BF)
    sent = dot(scatter, mixed).astype(BF)
    for k, sent_ref in enumerate(sent_refs):
        sent_ref[...] = sent[k * size : (k + 1) * size]


def ensemble_kernel(first, count, tile, feat_ref, w_ref, bias_ref, out_ref, after_ref, *refs):
    held = (len(refs) - 1) // 2
    copies = start_all(list(zip(refs[:held], refs[held + 1 :])), refs[-1]) if held else []
    pred_ref = refs[held]
    for t in range(count):
        rows = feat_ref[(first + t) * tile : (first + t + 1) * tile]
        total = None
        for m in range(w_ref.shape[0]):
            hidden = gelu2(dot(rows, w_ref[m]) + bias_ref[m : m + 1]).astype(BF)
            weights = jnp.broadcast_to(out_ref[m : m + 1].astype(F32), (8, out_ref.shape[1])).astype(BF)
            pred = dot_t(weights, hidden)[0:1]
            total = pred if total is None else total + pred
        per = tile // LANES
        for i in range(per):
            pred_ref[t * per + i : t * per + i + 1, :] = total[:, i * LANES : (i + 1) * LANES]
    for copy in copies:
        copy.wait()


def unpack(ref):
    depth = ref.shape[0] - EXTRA
    extra = ref[depth:, :].astype(F32)
    return ref[:depth, :], *(jnp.sum(extra[i : i + 3], axis=0, keepdims=True) for i in (DOWN, BIAS, HEAD))


def hidden_terms(normed, up, down, bias):
    return jnp.maximum(dot(normed, up) + bias, 0.0).astype(BF).astype(F32) * down


def states(mixed, table_ref, both0_ref, both1_ref):
    local = mixed.shape[1] // 2
    ow0, ow1 = (ref[ref.shape[0] - local :] for ref in (both0_ref, both1_ref))
    state = table_ref[CLS : CLS + 1, :] + dot(mixed[:, :local], ow0) + dot(mixed[:, local:], ow1)
    centered = centre(state)
    return state, (centered * inverse_spread(centered) * table_ref[FGAIN : FGAIN + 1, :]).astype(BF)


def arrived(got_refs, half, e):
    if len(got_refs) == 1:
        rows = got_refs[0].shape[0] // 2
        return got_refs[0][e * rows : (e + 1) * rows]
    return jnp.concatenate([ref[e * half : (e + 1) * half] for ref in got_refs], axis=0)


def arrive_kernel(blocks, half, *refs):
    table_ref, both0_ref, both1_ref, state_ref, normed_ref = refs[blocks:]
    state_ref[...], normed_ref[...] = states(arrived(refs[:blocks][::-1], half, 1), table_ref, both0_ref, both1_ref)


def near_score_kernel(blocks, half, *refs):
    table_ref, both0_ref, both1_ref, up0_ref, up1_ref, score_ref = refs[blocks:]
    state, normed = states(arrived(refs[:blocks][::-1], half, 0), table_ref, both0_ref, both1_ref)
    up, down, bias, head = unpack(up0_ref)
    terms = state * head + hidden_terms(normed, up, down, bias)
    up, down, bias, _ = unpack(up1_ref)
    terms = terms + hidden_terms(normed, up, down, bias)
    score_ref[...] = jnp.sum(terms, axis=-1, keepdims=True)


def far_score_kernel(blocks, half, near_ref, state_ref, mine_ref, other_ref, up2_ref, out_ref):
    rows = near_ref.shape[0]
    up, down, bias, head = unpack(up2_ref)
    terms = hidden_terms(jnp.concatenate([mine_ref[...], other_ref[...]], axis=0), up, down, bias)
    scores = [
        near_ref[...],
        jnp.sum(terms[:rows] + state_ref[...] * head, axis=-1, keepdims=True),
        jnp.sum(terms[rows:], axis=-1, keepdims=True),
    ]
    if blocks == 1:
        eye = iota((rows, rows), 0) == iota((rows, rows), 1)
        for e, score in enumerate(scores):
            out_ref[:, e * rows : (e + 1) * rows] = jnp.sum(jnp.where(eye, score, 0.0), axis=0, keepdims=True)
    else:
        row, lane = iota((half, LANES), 0), iota((half, LANES), 1)
        for k in range(blocks):
            line = jnp.zeros((half, LANES), F32)
            for e, score in enumerate(scores):
                line = jnp.where(lane == row + e * half, score[k * half : (k + 1) * half], line)
            out_ref[k : k + 1, :] = jnp.sum(line, axis=0, keepdims=True)


def expand_kernel(lines, where_ref, after_ref, line_ref, lane_ref):
    rows = lane_ref.shape[1]
    hit = where_ref[:, 2:3] == iota((where_ref.shape[0], rows), 1)

    def by_row(i):
        return jnp.sum(jnp.where(hit, where_ref[:, i : i + 1] + 1, 0).astype(F32), axis=0, keepdims=True).astype(jnp.int32)

    line = (by_row(0) - 1 == iota((lines, rows), 0)).astype(F32)
    line_ref[...] = jnp.concatenate([line] * 3, axis=0).astype(BF)
    lane_ref[...] = by_row(1) - 1


def finish_kernel(members, half, lines, line_ref, lane_ref, near_ref, far_ref, out_ref):
    near, far = near_ref[...], far_ref[...]
    ensemble = (near[lines:] + far[lines:]) * (0.5 / members)
    ensemble = jnp.concatenate([ensemble[i : i + 1] for i in range(ensemble.shape[0])], axis=1)
    lanes = iota((lines, LANES), 1)
    last = (lanes >= half) & (lanes < 2 * half)

    def whole(mine, others):
        return mine[:lines] + jnp.where(last, pltpu.roll(others[:lines], LANES - half, 1), 0.0)

    table = split3(jnp.concatenate([whole(near, far), whole(far, near)], axis=0))
    by_lane = lax.dot_general(table, line_ref[...], (((0,), (0,)), ((), ())), preferred_element_type=F32)
    lane = lane_ref[...]
    replaced = jnp.sum(jnp.where(lane == iota(by_lane.shape, 0), by_lane, 0.0), axis=0, keepdims=True)
    out_ref[...] = jnp.where(lane >= 0, replaced, ensemble)


def cost(flops, size, trans=0):
    return pl.CostEstimate(flops=flops, bytes_accessed=size, transcendentals=trans)


def params(mib):
    return pltpu.CompilerParams(vmem_limit_bytes=mib * 2**20)


def in_hbm(arrays):
    return [pltpu.with_memory_space_constraint(x, pltpu.HBM) for x in arrays]


def shape(dims, dtype):
    return jax.ShapeDtypeStruct(dims, dtype)


def per_device(
    features, escalated, owner_ids, member_in, member_bias, member_out, feat_weight, feat_bias,
    pred_scale, pred_shift, cls_token, attn_gain, qkv_weight, out_weight, ffn_gain, up_weight,
    up_bias, down_weight, owner_heads,
):
    n = lax.axis_size("rows")
    rows, fwidth = features.shape
    count = escalated.shape[1]
    half = max(1, count // n)
    slots = n * half
    here, _, hidden = member_in.shape
    members = pred_scale.shape[0]
    width = cls_token.shape[0]

    def swap(x):
        return lax.ppermute(x, "member", [(0, 1), (1, 0)])

    row = lambda x: x.reshape(1, -1)
    cls_token, attn_gain, ffn_gain, feat_bias = map(row, (cls_token, attn_gain, ffn_gain, feat_bias))
    owners = owner_ids.reshape(1, count)

    pairs = n // 2
    relative = pairs <= 8
    blocks = pairs if relative else 1
    other_qkv = swap(qkv_weight)

    dealt = count // 2
    ins = (escalated, owners, features, down_weight, up_weight, feat_weight, out_weight)
    index, mine, down, segment, own_both = pl.pallas_call(
        functools.partial(route_kernel, n, half, relative),
        out_shape=[shape((8, count), jnp.int32), shape((count, fwidth), BF), shape(down_weight.shape[1:], BF),
                   shape((up_weight.shape[1] + EXTRA, up_weight.shape[2]), BF),
                   shape((feat_weight.shape[0] + out_weight.shape[0], width), BF)],
        in_specs=[HBM] * len(ins),
        out_specs=[VMEM] * 5,
        scratch_shapes=[pltpu.VMEM(x.shape, x.dtype) for x in ins[:3]] + [pltpu.SemaphoreType.DMA((7,))],
        compiler_params=params(24),
        cost_estimate=cost(2 * count * rows * fwidth, 3 * 10**6),
        name="route",
    )(*in_hbm(ins))
    near, far, segment = pl.pallas_call(
        predict_kernel,
        out_shape=[shape((dealt, 8), BF), shape((dealt, 8), BF), shape(segment.shape, BF)],
        in_specs=[VMEM] * 8,
        out_specs=[VMEM] * 3,
        input_output_aliases={7: 2},
        compiler_params=params(24),
        cost_estimate=cost(2 * here * count * fwidth * hidden, 3 * 10**6, here * count * hidden),
        name="predict",
    )(mine, member_in, member_bias, member_out, up_bias, owner_heads, down, segment)
    far = swap(far)
    other_both = swap(own_both)
    next_segment = lax.ppermute(segment, "rows", [(i, i ^ 1) for i in range(n)])
    other_segment = swap(segment)

    ins = (cls_token, attn_gain, pred_scale, pred_shift, feat_bias, ffn_gain, qkv_weight, other_qkv, index)
    table, where, place = pl.pallas_call(
        constants_kernel,
        out_shape=[shape((TABLE, width), F32), shape((count, 3), jnp.int32), shape((1, dealt), jnp.int32)],
        in_specs=[VMEM] * len(ins),
        out_specs=[VMEM] * 3,
        compiler_params=params(16),
        cost_estimate=cost(10**8, 2 * 10**6),
        name="constants",
    )(*ins)

    local = qkv_weight.shape[2]
    sent = pl.pallas_call(
        functools.partial(attend_kernel, members),
        out_shape=[shape((slots // blocks, 2 * local), BF)] * blocks,
        in_specs=[VMEM] * 9,
        out_specs=[VMEM] * blocks,
        compiler_params=params(24),
        cost_estimate=cost(10**9, 2 * 10**6),
        name="attend",
    )(mine, near, far, place, table, own_both, other_both, qkv_weight, other_qkv)

    def across(x, k):
        return lax.ppermute(x, "rows", [(i, i ^ (2 * k)) for i in range(n)])

    def exchange(x):
        groups = [[2 * q + b for q in range(pairs)] for b in range(2)]
        return lax.all_to_all(x, "rows", split_axis=0, concat_axis=0, axis_index_groups=groups, tiled=True)

    if relative:
        got = [sent[0]] + [across(sent[k], k) for k in range(1, pairs)]
    else:
        got = exchange(sent[0].reshape(pairs, 2, half, 2 * local))
        got = [got.transpose(1, 0, 2, 3).reshape(slots, 2 * local)]

    tile = min(rows, 256)
    tiles = rows // tile

    def ensemble(first, number, after, held=()):
        return pl.pallas_call(
            functools.partial(ensemble_kernel, first, number, tile),
            out_shape=[shape((number * tile // LANES, LANES), F32)] + [shape(x.shape, x.dtype) for x in held],
            in_specs=[VMEM] * 4 + [ANY] * (1 + len(held)),
            out_specs=[VMEM] * (1 + len(held)),
            scratch_shapes=[pltpu.SemaphoreType.DMA((len(held),))] if held else [],
            compiler_params=params(24),
            cost_estimate=cost(2 * here * number * tile * fwidth * hidden, 10**6, here * number * tile * hidden),
            name="ensemble",
        )(features, member_in, member_bias, member_out, after, *held)

    early = (tiles + 1) // 2
    preds, table, both0, both1, up0, up1 = ensemble(
        0, early, sent[0], (table, own_both, other_both, segment, other_segment))
    preds = [preds]

    state, next_rows = pl.pallas_call(
        functools.partial(arrive_kernel, blocks, half),
        out_shape=[shape((slots // 2, width), F32), shape((slots // 2, width), BF)],
        in_specs=[VMEM] * (blocks + 3),
        out_specs=[VMEM] * 2,
        compiler_params=params(24),
        cost_estimate=cost(2 * 10**8, 2 * 10**6),
        name="arrive",
    )(*got[::-1], table, both0, both1)
    other_rows = swap(next_rows)
    near_scores = pl.pallas_call(
        functools.partial(near_score_kernel, blocks, half),
        out_shape=shape((slots // 2, 1), F32),
        in_specs=[VMEM] * (blocks + 5),
        out_specs=VMEM,
        compiler_params=params(24),
        cost_estimate=cost(5 * 10**8, 2 * 10**6),
        name="near_score",
    )(*got[::-1], table, both0, both1, up0, up1)
    scores = pl.pallas_call(
        functools.partial(far_score_kernel, blocks, half),
        out_shape=shape((blocks, LANES if relative else 3 * slots // 2), F32),
        in_specs=[VMEM] * 5,
        out_specs=VMEM,
        compiler_params=params(24),
        cost_estimate=cost(2 * 10**8, 10**6),
        name="far_score",
    )(near_scores, state, next_rows, other_rows, next_segment)
    for first in range(early, tiles):
        preds += ensemble(first, 1, scores)
    back = scores
    if relative:
        step = 1
        while step < pairs:
            back = jnp.concatenate([back, across(back, step)], axis=0)
            step *= 2
    else:
        back = exchange(back.reshape(3, pairs, half).transpose(1, 0, 2)).reshape(pairs, 3 * half)
        back = jnp.pad(back, ((0, 0), (0, LANES - 3 * half)))
    lines = back.shape[0]
    near_lines = jnp.concatenate([back, *preds], axis=0)
    line_of, lane_of = pl.pallas_call(
        functools.partial(expand_kernel, 2 * lines),
        out_shape=[shape((6 * lines, rows), BF), shape((1, rows), jnp.int32)],
        in_specs=[VMEM, ANY],
        out_specs=[VMEM] * 2,
        compiler_params=params(16),
        cost_estimate=cost(10**8, 10**6),
        name="expand",
    )(where, preds[-1])

    final = pl.pallas_call(
        functools.partial(finish_kernel, members, half, lines),
        out_shape=shape((1, rows), F32),
        in_specs=[VMEM] * 4,
        out_specs=VMEM,
        compiler_params=params(8),
        cost_estimate=cost(10**6, 10**6),
        name="finish",
    )(line_of, lane_of, near_lines, swap(near_lines))
    return final.reshape(rows)


def solution(mesh):
    placed = (
        P(("groups", "rows"), None),
        P(("groups", "rows"), None),
        P(("groups", "rows"), None, None),
        P("member", None, None),
        P("member", None),
        P("member", None),
        P("member", None),
        P(),
        P(),
        P(),
        P(),
        P(),
        P(None, None, "member"),
        P("member", None),
        P(),
        P("rows", None, "member"),
        P("rows", "member"),
        P("rows", "member", None),
        P("rows", None),
    )
    return jax.shard_map(
        per_device, mesh=mesh, in_specs=placed, out_specs=P(("groups", "rows")), check_vma=False
    )
```

profile of v0, /device:TPU:0, one launch (start us, length us, event | category | flops | bytes accessed | tf_op | source)
XLA Modules:
  0.0 32.6 jit_solution(6314064323378376487)
XLA Ops:
  0.0 0.5 %collective-permute-start = (bf16[3,512,256]{2,1,0:T(8,128)(2,1)}, bf16[3,512,256]{2,1,0:T(8,128)(2,1)S(1)}, u32[]{:S(2)}, u32[]{:S(2)}) collective-permute-start(bf16[3,512,256]{2,1,0:T(8,128)(2,1)} %q0_ref.3), channel_id=1, source_target_pairs={{0,1},{1,0},{2,3},{3,2},{4,5},{5,4},{6,7},{7,6},{8,9},{9,8},{10,11... | collective-permute-start | bytes 2359304 | tf_op jit(solution)/shard_map/ppermute | solution.py:377
  0.5 1.9 %route.1 = (s32[8,256]{1,0:T(8,128)S(1)}, bf16[256,512]{1,0:T(8,128)(2,1)S(1)}, bf16[512,512]{1,0:T(8,128)(2,1)S(1)}, bf16[528,512]{1,0:T(8,128)(2,1)S(1)}, bf16[512,512]{1,0:T(8,128)(2,1)S(1)}) custom-call(s32[1,256]{1,0:T(1,128)} %esc_hbm.1, s32[1,256]{1,0:T(1,128)} %bitcast.10, bf16[1024,512]{1,0:T(8,128)(2,1)} %feat_ref.5, ...), custom_call_target="tpu_custom_call" | custom-call | flops 268435456 | bytes 3000000 | tf_op jit(solution)/shard_map/route/pallas_call | solution.py:390
  2.7 1.3 %predict.1 = (bf16[128,8]{1,0:T(8,128)(2,1)S(1)}, bf16[128,8]{1,0:T(8,128)(2,1)S(1)}, bf16[528,512]{1,0:T(8,128)(2,1)S(1)}) custom-call(bf16[256,512]{1,0:T(8,128)(2,1)S(1)} %get-tuple-element.32.rows_ref, bf16[2,512,1024]{2,1,0:T(8,128)(2,1)S(1)} %copy-done, f32[2,1024]{1,0:T(2,128)S(1)} %copy-done.3, ...), custom_call_target="tpu_custom_call", output_to_operand_aliasing={{2}: (7, {})} | custom-call | flops 536870912 | bytes 3000000 | tf_op jit(solution)/shard_map/predict/pallas_call | solution.py:402
  4.0 0.5 %collective-permute-start.6 = (bf16[528,512]{1,0:T(8,128)(2,1)S(1)}, bf16[528,512]{1,0:T(8,128)(2,1)S(1)}, u32[]{:S(2)}, u32[]{:S(2)}) collective-permute-start(bf16[528,512]{1,0:T(8,128)(2,1)S(1)} %get-tuple-element.44.refs_3_), channel_id=1, source_target_pairs={{0,1},{1,0},{2,3},{3,2},{4,5},{5,4},{6,7},{7,6},{8,9},{9,8},{10,11... | collective-permute-start | bytes 1622024 | tf_op jit(solution)/shard_map/ppermute | solution.py:377
  4.5 2.5 %collective-permute-start.8 = (bf16[528,512]{1,0:T(8,128)(2,1)S(1)}, bf16[528,512]{1,0:T(8,128)(2,1)S(1)}, u32[]{:S(2)}, u32[]{:S(2)}) collective-permute-start(bf16[528,512]{1,0:T(8,128)(2,1)S(1)} %get-tuple-element.44.refs_3_), channel_id=1, source_target_pairs={{0,2},{2,0},{4,6},{6,4},{8,10},{10,8},{12,14},{14,12},{1,3},{3,1},... | collective-permute-start | bytes 1622024 | tf_op jit(solution)/shard_map/ppermute | solution.py:414
  7.2 0.7 %constants.1 = (f32[40,512]{1,0:T(8,128)S(1)}, s32[256,3]{1,0:T(8,128)S(1)}, s32[1,128]{1,0:T(1,128)S(1)}) custom-call(f32[1,512]{1,0:T(1,128)S(1)} %bitcast.6, f32[1,512]{1,0:T(1,128)S(1)} %bitcast.7, f32[4,512]{1,0:T(4,128)S(1)} %copy-done.5, f32[4,512]{1,0:T(4,128)S(1)} %copy-done.6, f32[1,512]{1,0:T(1,128)S(1)} %bitcast.8, f32[1,512]{1,0:T(1,128)S(1)} %bitcast.9, ...), custom_call_target="tpu_custom_call" | custom-call | flops 100000000 | bytes 2000000 | tf_op jit(solution)/shard_map/constants/pallas_call | solution.py:418
  8.2 2.1 %attend.1 = (bf16[64,512]{1,0:T(8,128)(2,1)S(1)}, bf16[64,512]{1,0:T(8,128)(2,1)S(1)}, bf16[64,512]{1,0:T(8,128)(2,1)S(1)}, bf16[64,512]{1,0:T(8,128)(2,1)S(1)}) custom-call(bf16[256,512]{1,0:T(8,128)(2,1)S(1)} %get-tuple-element.32.rows_ref, bf16[128,8]{1,0:T(8,128)(2,1)S(1)} %get-tuple-element.35.near_ref, ...), custom_call_target="tpu_custom_call" | custom-call | flops 1000000000 | bytes 2000000 | tf_op jit(solution)/shard_map/attend/pallas_call | solution.py:429
  10.4 3.7 %collective-permute-start.3 = (bf16[64,512]{1,0:T(8,128)(2,1)S(1)}, bf16[64,512]{1,0:T(8,128)(2,1)S(1)}, u32[]{:S(2)}, u32[]{:S(2)}) collective-permute-start(bf16[64,512]{1,0:T(8,128)(2,1)S(1)} %get-tuple-element.40), channel_id=1, source_target_pairs={{0,12},{2,14},{4,8},{6,10},{8,4},{10,6},{12,0},{14,2},{1,13},{3,15... | collective-permute-start | bytes 196616 | tf_op jit(solution)/shard_map/ppermute | solution.py:440
  14.0 0.8 %collective-permute-start.5 = (bf16[64,512]{1,0:T(8,128)(2,1)S(1)}, bf16[64,512]{1,0:T(8,128)(2,1)S(1)}, u32[]{:S(2)}, u32[]{:S(2)}) collective-permute-start(bf16[64,512]{1,0:T(8,128)(2,1)S(1)} %get-tuple-element.42), channel_id=1, source_target_pairs={{0,4},{2,6},{4,0},{6,2},{8,12},{10,14},{12,8},{14,10},{1,5},{3,7},... | collective-permute-start | bytes 196616 | tf_op jit(solution)/shard_map/ppermute | solution.py:440
  14.8 2.4 %ensemble.3 = (f32[4,128]{1,0:T(4,128)S(1)}, f32[40,512]{1,0:T(8,128)S(1)}, bf16[512,512]{1,0:T(8,128)(2,1)S(1)}, bf16[512,512]{1,0:T(8,128)(2,1)S(1)}, bf16[528...) custom-call(bf16[1024,512]{1,0:T(8,128)(2,1)S(1)} %copy-done.1, bf16[2,512,1024]{2,1,0:T(8,128)(2,1)S(1)} %copy-done, ...), custom_call_target="tpu_custom_call" | custom-call | flops 1073741824 | bytes 1000000 | tf_op jit(solution)/shard_map/ensemble/pallas_call | solution.py:456
  17.2 2.7 %collective-permute-done.4.refs_1_ = bf16[64,512]{1,0:T(8,128)(2,1)S(1)} collective-permute-done((bf16[64,512]{1,0:T(8,128)(2,1)S(1)}, bf16[64,512]{1,0:T(8,128)(2,1)S(1)}, u32[]{:S(2)}, u32[]{:S(2)}) %collective-permute-start.4) | collective-permute-done | bytes 65568 | tf_op jit(solution)/shard_map/ppermute | solution.py:440
  19.9 0.4 %arrive.1 = (f32[128,512]{1,0:T(8,128)S(1)}, bf16[128,512]{1,0:T(8,128)(2,1)S(1)}) custom-call(bf16[64,512]{1,0:T(8,128)(2,1)S(1)} %collective-permute-done.3.refs_0_, bf16[64,512]{1,0:T(8,128)(2,1)S(1)} %collective-permute-done.4.refs_1_, bf16[64,512]{1,0:T(8,128)(2,1)S(1)} %collective-permute-done.5.refs_2_, ...), custom_call_target="tpu_custom_call" | custom-call | flops 200000000 | bytes 2000000 | tf_op jit(solution)/shard_map/arrive/pallas_call | solution.py:472
  20.4 0.8 %near_score.1.near_ref = f32[128,1]{1,0:T(8,128)S(1)} custom-call(bf16[64,512]{1,0:T(8,128)(2,1)S(1)} %collective-permute-done.3.refs_0_, bf16[64,512]{1,0:T(8,128)(2,1)S(1)} %collective-permute-done.4.refs_1_, bf16[64,512]{1,0:T(8,128)(2,1)S(1)} %collective-permute-done.5.refs_2_, bf16[64,512]{1,0:T(8,128)(2,1)S(1)} %get-tuple-element.43.after_ref.refs_3_, ...), custom_call_target="tpu_custom_call" | custom-call | flops 500000000 | bytes 2000000 | tf_op jit(solution)/shard_map/near_score/pallas_call | solution.py:482
  21.2 0.6 %collective-permute-done.7.other_ref = bf16[128,512]{1,0:T(8,128)(2,1)S(1)} collective-permute-done((bf16[128,512]{1,0:T(8,128)(2,1)S(1)}, bf16[128,512]{1,0:T(8,128)(2,1)S(1)}, u32[]{:S(2)}, u32[]{:S(2)}) %collective-permute-start.7) | collective-permute-done | bytes 131104 | tf_op jit(solution)/shard_map/ppermute | solution.py:377
  21.8 0.4 %far_score.1.after_ref = f32[4,128]{1,0:T(4,128)S(1)} custom-call(f32[128,1]{1,0:T(8,128)S(1)} %near_score.1.near_ref, f32[128,512]{1,0:T(8,128)S(1)} %get-tuple-element.50.state_ref, bf16[128,512]{1,0:T(8,128)(2,1)S(1)} %get-tuple-element.51.mine_ref, bf16[128,512]{1,0:T(8,128)(2,1)S(1)} %collective-permute-done.7.other_ref, ...), custom_call_target="tpu_custom_call" | custom-call | flops 200000000 | bytes 1000000 | tf_op jit(solution)/shard_map/far_score/pallas_call | solution.py:491
  22.2 1.2 %collective-permute-start.9 = (f32[4,128]{1,0:T(4,128)S(1)}, f32[4,128]{1,0:T(4,128)S(1)}, u32[]{:S(2)}, u32[]{:S(2)}) collective-permute-start(f32[4,128]{1,0:T(4,128)S(1)} %far_score.1.after_ref), channel_id=1, source_target_pairs={{0,4},{2,6},{4,0},{6,2},{8,12},{10,14},{12,8},{14,10},{1,5},{3,7},... | collective-permute-start | bytes 6152 | tf_op jit(solution)/shard_map/ppermute | solution.py:440
  23.4 1.1 %ensemble.4.after_ref = f32[2,128]{1,0:T(2,128)S(1)} custom-call(bf16[1024,512]{1,0:T(8,128)(2,1)S(1)} %copy-done.1, bf16[2,512,1024]{2,1,0:T(8,128)(2,1)S(1)} %copy-done, f32[2,1024]{1,0:T(2,128)S(1)} %copy-done.3, bf16[2,1024]{1,0:T(2,128)(2,1)S(1)} %copy-done.4, f32[4,128]{1,0:T(4,128)S(1)} %far_score.1.after_ref), custom_call_target="tpu_custom_call" | custom-call | flops 536870912 | bytes 1000000 | tf_op jit(solution)/shard_map/ensemble/pallas_call | solution.py:456
  24.5 1.3 %collective-permute-done.9 = f32[4,128]{1,0:T(4,128)S(1)} collective-permute-done((f32[4,128]{1,0:T(4,128)S(1)}, f32[4,128]{1,0:T(4,128)S(1)}, u32[]{:S(2)}, u32[]{:S(2)}) %collective-permute-start.9) | collective-permute-done | bytes 2080 | tf_op jit(solution)/shard_map/ppermute | solution.py:440
  25.8 1.3 %collective-permute-start.10 = (f32[8,128]{1,0:T(8,128)S(1)}, f32[8,128]{1,0:T(8,128)S(1)}, u32[]{:S(2)}, u32[]{:S(2)}) collective-permute-start(f32[8,128]{1,0:T(8,128)S(1)} %pad_maximum_fusion), channel_id=1, source_target_pairs={{0,8},{2,10},{4,12},{6,14},{8,0},{10,2},{12,4},{14,6},{1,9},{3,11}... | collective-permute-start | bytes 12296 | tf_op jit(solution)/shard_map/ppermute | solution.py:440
  27.2 1.1 %ensemble.5 = f32[2,128]{1,0:T(2,128)S(1)} custom-call(bf16[1024,512]{1,0:T(8,128)(2,1)S(1)} %copy-done.1, bf16[2,512,1024]{2,1,0:T(8,128)(2,1)S(1)} %copy-done, f32[2,1024]{1,0:T(2,128)S(1)} %copy-done.3, bf16[2,1024]{1,0:T(2,128)(2,1)S(1)} %copy-done.4, f32[4,128]{1,0:T(4,128)S(1)} %far_score.1.after_ref), custom_call_target="tpu_custom_call" | custom-call | flops 536870912 | bytes 1000000 | tf_op jit(solution)/shard_map/ensemble/pallas_call | solution.py:456
  28.3 2.0 %collective-permute-done.10 = f32[8,128]{1,0:T(8,128)S(1)} collective-permute-done((f32[8,128]{1,0:T(8,128)S(1)}, f32[8,128]{1,0:T(8,128)S(1)}, u32[]{:S(2)}, u32[]{:S(2)}) %collective-permute-start.10) | collective-permute-done | bytes 4128 | tf_op jit(solution)/shard_map/ppermute | solution.py:440
  30.5 0.4 %expand.1 = (bf16[96,1024]{1,0:T(8,128)(2,1)S(1)}, s32[1,1024]{1,0:T(1,128)S(1)}) custom-call(s32[256,3]{1,0:T(8,128)S(1)} %get-tuple-element.31.where_ref, f32[2,128]{1,0:T(2,128)S(1)} %ensemble.4.after_ref), custom_call_target="tpu_custom_call" | custom-call | flops 100000000 | bytes 1000000 | tf_op jit(solution)/shard_map/expand/pallas_call | solution.py:513
  30.9 0.7 %collective-permute-done.11.far_ref = f32[24,128]{1,0:T(8,128)S(1)} collective-permute-done((f32[24,128]{1,0:T(8,128)S(1)}, f32[24,128]{1,0:T(8,128)S(1)}, u32[]{:S(2)}, u32[]{:S(2)}) %collective-permute-start.11) | collective-permute-done | bytes 12320 | tf_op jit(solution)/shard_map/ppermute | solution.py:377
  31.6 0.9 %finish.1 = f32[1,1024]{1,0:T(1,128)} custom-call(bf16[96,1024]{1,0:T(8,128)(2,1)S(1)} %get-tuple-element.52.line_ref, s32[1,1024]{1,0:T(1,128)S(1)} %get-tuple-element.53.lane_ref, f32[24,128]{1,0:T(8,128)S(1)} %concatenate.8.near_ref, f32[24,128]{1,0:T(8,128)S(1)} %collective-permute-done.11.far_ref), custom_call_target="tpu_custom_call" | custom-call | flops 1000000 | bytes 1000000 | tf_op jit(solution)/shard_map/finish/pallas_call | solution.py:523
  (40 shorter events, 0.7 us)
Async XLA Ops:
  0.0 2.6 %copy-start.3 = (f32[2,1024]{1,0:T(2,128)S(1)}, f32[2,1024]{1,0:T(2,128)}, u32[]{:S(2)}) copy-start(f32[2,1024]{1,0:T(2,128)} %bias_ref.7) | copy-start | bytes 24580
  0.0 2.6 %copy-start.4 = (bf16[2,1024]{1,0:T(2,128)(2,1)S(1)}, bf16[2,1024]{1,0:T(2,128)(2,1)}, u32[]{:S(2)}) copy-start(bf16[2,1024]{1,0:T(2,128)(2,1)} %out_ref.7) | copy-start | bytes 12292
  0.0 2.7 %copy-start.11 = (f32[1,512]{1,0:T(1,128)S(1)}, f32[1,512]{1,0:T(1,128)}, u32[]{:S(2)}) copy-start(f32[1,512]{1,0:T(1,128)} %upb_ref.1) | copy-start | bytes 6148
  0.0 2.7 %copy-start.12 = (f32[1,512]{1,0:T(1,128)S(1)}, f32[1,512]{1,0:T(1,128)}, u32[]{:S(2)}) copy-start(f32[1,512]{1,0:T(1,128)} %head_ref.1) | copy-start | bytes 6148
  0.0 7.1 %collective-permute-start = (bf16[3,512,256]{2,1,0:T(8,128)(2,1)}, bf16[3,512,256]{2,1,0:T(8,128)(2,1)S(1)}, u32[]{:S(2)}, u32[]{:S(2)}) collective-permute-start(bf16[3,512,256]{2,1,0:T(8,128)(2,1)} %q0_ref.3), channel_id=1, source_target_pairs={{0,1},{1,0},{2,3},{3,2},{4,5},{5,4},{6,7},{7,6},{8,9},{9,8},{10,11... | collective-permute-start | bytes 2359304 | tf_op jit(solution)/shard_map/ppermute | solution.py:377
  2.5 4.6 %copy-start.2 = (bf16[3,512,256]{2,1,0:T(8,128)(2,1)S(1)}, bf16[3,512,256]{2,1,0:T(8,128)(2,1)}, u32[]{:S(2)}) copy-start(bf16[3,512,256]{2,1,0:T(8,128)(2,1)} %q0_ref.3) | copy-start | bytes 2359300
  2.5 4.6 %copy-start.5 = (f32[4,512]{1,0:T(4,128)S(1)}, f32[4,512]{1,0:T(4,128)}, u32[]{:S(2)}) copy-start(f32[4,512]{1,0:T(4,128)} %scale_ref.1) | copy-start | bytes 24580
  2.5 4.6 %copy-start.6 = (f32[4,512]{1,0:T(4,128)S(1)}, f32[4,512]{1,0:T(4,128)}, u32[]{:S(2)}) copy-start(f32[4,512]{1,0:T(4,128)} %shift_ref.1) | copy-start | bytes 24580
  2.5 4.6 %copy-start.7 = (f32[512]{0:T(512)S(1)}, f32[512]{0:T(512)}, u32[]{:S(2)}) copy-start(f32[512]{0:T(512)} %param.29) | copy-start | bytes 6148
  2.5 4.6 %copy-start.8 = (f32[512]{0:T(512)S(1)}, f32[512]{0:T(512)}, u32[]{:S(2)}) copy-start(f32[512]{0:T(512)} %param.30) | copy-start | bytes 6148
  2.5 4.6 %copy-start.9 = (f32[512]{0:T(512)S(1)}, f32[512]{0:T(512)}, u32[]{:S(2)}) copy-start(f32[512]{0:T(512)} %param.26) | copy-start | bytes 6148
  2.5 4.6 %copy-start.10 = (f32[512]{0:T(512)S(1)}, f32[512]{0:T(512)}, u32[]{:S(2)}) copy-start(f32[512]{0:T(512)} %param.33) | copy-start | bytes 6148
  2.6 5.7 %collective-permute-start.2 = (bf16[512,512]{1,0:T(8,128)(2,1)S(1)}, bf16[512,512]{1,0:T(8,128)(2,1)S(1)}, u32[]{:S(2)}, u32[]{:S(2)}) collective-permute-start(bf16[512,512]{1,0:T(8,128)(2,1)S(1)} %get-tuple-element.39.fw0_ref.refs_1_), channel_id=1, source_target_pairs={{0,1},{1,0},{2,3},{3,2},{4,5},{5,4},{6,7},{7,6},{8,9},{9,8},{10,11... | collective-permute-start | bytes 1572872 | tf_op jit(solution)/shard_map/ppermute | solution.py:377
  4.0 10.8 %collective-permute-start.6 = (bf16[528,512]{1,0:T(8,128)(2,1)S(1)}, bf16[528,512]{1,0:T(8,128)(2,1)S(1)}, u32[]{:S(2)}, u32[]{:S(2)}) collective-permute-start(bf16[528,512]{1,0:T(8,128)(2,1)S(1)} %get-tuple-element.44.refs_3_), channel_id=1, source_target_pairs={{0,1},{1,0},{2,3},{3,2},{4,5},{5,4},{6,7},{7,6},{8,9},{9,8},{10,11... | collective-permute-start | bytes 1622024 | tf_op jit(solution)/shard_map/ppermute | solution.py:377
  4.5 16.7 %collective-permute-start.8 = (bf16[528,512]{1,0:T(8,128)(2,1)S(1)}, bf16[528,512]{1,0:T(8,128)(2,1)S(1)}, u32[]{:S(2)}, u32[]{:S(2)}) collective-permute-start(bf16[528,512]{1,0:T(8,128)(2,1)S(1)} %get-tuple-element.44.refs_3_), channel_id=1, source_target_pairs={{0,2},{2,0},{4,6},{6,4},{8,10},{10,8},{12,14},{14,12},{1,3},{3,1},... | collective-permute-start | bytes 1622024 | tf_op jit(solution)/shard_map/ppermute | solution.py:414
  7.0 1.2 %collective-permute-start.1 = (bf16[128,8]{1,0:T(8,128)(2,1)S(1)}, bf16[128,8]{1,0:T(8,128)(2,1)S(1)}, u32[]{:S(2)}, u32[]{:S(2)}) collective-permute-start(bf16[128,8]{1,0:T(8,128)(2,1)S(1)} %get-tuple-element.36), channel_id=1, source_target_pairs={{0,1},{1,0},{2,3},{3,2},{4,5},{5,4},{6,7},{7,6},{8,9},{9,8},{10,11... | collective-permute-start | bytes 6152 | tf_op jit(solution)/shard_map/ppermute | solution.py:377
  7.9 6.9 %copy-start.1 = (bf16[1024,512]{1,0:T(8,128)(2,1)S(1)}, bf16[1024,512]{1,0:T(8,128)(2,1)}, u32[]{:S(2)}) copy-start(bf16[1024,512]{1,0:T(8,128)(2,1)} %feat_ref.5) | copy-start | bytes 3145732
  10.4 6.9 %collective-permute-start.3 = (bf16[64,512]{1,0:T(8,128)(2,1)S(1)}, bf16[64,512]{1,0:T(8,128)(2,1)S(1)}, u32[]{:S(2)}, u32[]{:S(2)}) collective-permute-start(bf16[64,512]{1,0:T(8,128)(2,1)S(1)} %get-tuple-element.40), channel_id=1, source_target_pairs={{0,12},{2,14},{4,8},{6,10},{8,4},{10,6},{12,0},{14,2},{1,13},{3,15... | collective-permute-start | bytes 196616 | tf_op jit(solution)/shard_map/ppermute | solution.py:440
  14.0 5.9 %collective-permute-start.4 = (bf16[64,512]{1,0:T(8,128)(2,1)S(1)}, bf16[64,512]{1,0:T(8,128)(2,1)S(1)}, u32[]{:S(2)}, u32[]{:S(2)}) collective-permute-start(bf16[64,512]{1,0:T(8,128)(2,1)S(1)} %get-tuple-element.41), channel_id=1, source_target_pairs={{0,8},{2,10},{4,12},{6,14},{8,0},{10,2},{12,4},{14,6},{1,9},{3,11}... | collective-permute-start | bytes 196616 | tf_op jit(solution)/shard_map/ppermute | solution.py:440
  14.0 5.9 %collective-permute-start.5 = (bf16[64,512]{1,0:T(8,128)(2,1)S(1)}, bf16[64,512]{1,0:T(8,128)(2,1)S(1)}, u32[]{:S(2)}, u32[]{:S(2)}) collective-permute-start(bf16[64,512]{1,0:T(8,128)(2,1)S(1)} %get-tuple-element.42), channel_id=1, source_target_pairs={{0,4},{2,6},{4,0},{6,2},{8,12},{10,14},{12,8},{14,10},{1,5},{3,7},... | collective-permute-start | bytes 196616 | tf_op jit(solution)/shard_map/ppermute | solution.py:440
  20.3 1.4 %collective-permute-start.7 = (bf16[128,512]{1,0:T(8,128)(2,1)S(1)}, bf16[128,512]{1,0:T(8,128)(2,1)S(1)}, u32[]{:S(2)}, u32[]{:S(2)}) collective-permute-start(bf16[128,512]{1,0:T(8,128)(2,1)S(1)} %get-tuple-element.51.mine_ref), channel_id=1, source_target_pairs={{0,1},{1,0},{2,3},{3,2},{4,5},{5,4},{6,7},{7,6},{8,9},{9,8},{10,11... | collective-permute-start | bytes 393224 | tf_op jit(solution)/shard_map/ppermute | solution.py:377
  22.2 3.7 %collective-permute-start.9 = (f32[4,128]{1,0:T(4,128)S(1)}, f32[4,128]{1,0:T(4,128)S(1)}, u32[]{:S(2)}, u32[]{:S(2)}) collective-permute-start(f32[4,128]{1,0:T(4,128)S(1)} %far_score.1.after_ref), channel_id=1, source_target_pairs={{0,4},{2,6},{4,0},{6,2},{8,12},{10,14},{12,8},{14,10},{1,5},{3,7},... | collective-permute-start | bytes 6152 | tf_op jit(solution)/shard_map/ppermute | solution.py:440
  25.8 4.5 %collective-permute-start.10 = (f32[8,128]{1,0:T(8,128)S(1)}, f32[8,128]{1,0:T(8,128)S(1)}, u32[]{:S(2)}, u32[]{:S(2)}) collective-permute-start(f32[8,128]{1,0:T(8,128)S(1)} %pad_maximum_fusion), channel_id=1, source_target_pairs={{0,8},{2,10},{4,12},{6,14},{8,0},{10,2},{12,4},{14,6},{1,9},{3,11}... | collective-permute-start | bytes 12296 | tf_op jit(solution)/shard_map/ppermute | solution.py:440
  30.4 1.2 %collective-permute-start.11 = (f32[24,128]{1,0:T(8,128)S(1)}, f32[24,128]{1,0:T(8,128)S(1)}, u32[]{:S(2)}, u32[]{:S(2)}) collective-permute-start(f32[24,128]{1,0:T(8,128)S(1)} %concatenate.8.near_ref), channel_id=1, source_target_pairs={{0,1},{1,0},{2,3},{3,2},{4,5},{5,4},{6,7},{7,6},{8,9},{9,8},{10,11... | collective-permute-start | bytes 36872 | tf_op jit(solution)/shard_map/ppermute | solution.py:377
  (1 other events, 2.6 us)
where the time goes:
time: 32.7 us; the launch traced here: 32.6 us
  Pallas kernels  13.7 us (42%)
  starting transfers between devices  10.8 us (33%)
  waiting for transfers between devices  7.66 us (23%)
    ppermute x5, starting transfers between devices, across(): return lax.ppermute(x, 'rows', [(i, i ^ 2 * k) for i in range(n)])  6.97 us
    ppermute x5, waiting for transfers between devices, across(): return lax.ppermute(x, 'rows', [(i, i ^ 2 * k) for i in range(n)])  6.04 us
    pallas_call x3, Pallas kernels, ensemble(): pl.pallas_call(functools.partial(ensemble_kernel, first, number, tile), o...  4.68 us
    ppermute x1, starting transfers between devices, per_device(): next_segment = lax.ppermute(segment, 'rows', [(i, i ^ 1) for i in range(n)])  2.5 us
    pallas_call x1, Pallas kernels, per_device(): pl.pallas_call(functools.partial(attend_kernel, members), out_shape=[shap...  2.13 us
    pallas_call x1, Pallas kernels, per_device(): pl.pallas_call(functools.partial(route_kernel, n, half, relative), out_sh...  1.91 us
    ppermute x6, waiting for transfers between devices, swap(): return lax.ppermute(x, 'member', [(0, 1), (1, 0)])  1.62 us
    ppermute x6, starting transfers between devices, swap(): return lax.ppermute(x, 'member', [(0, 1), (1, 0)])  1.36 us
  transfers between devices with their start and end apart: 12, of which 6 were waited for; matrix products, arithmetic and copies ran while one was open for 0% of the time, Pallas kernels for 38%

commit v1 on v0

--- a/solution.py
+++ b/solution.py
@@ -20,7 +20,7 @@
 
 KMAP, VCLS, LCLS, SCALE, SHIFT, GAIN, FBIAS, CLS, FGAIN = 0, 8, 9, 16, 24, 32, 33, 34, 35
 TABLE = 40
-DOWN, BIAS, HEAD, EXTRA = 0, 3, 6, 16
+DOWN, BIAS, HEAD, PREDS, EXTRA = 0, 3, 6, 9, 16
 
 
 def iota(shape, dim):
@@ -114,27 +114,28 @@
 
 def predict_kernel(
     rows_ref, w_ref, bias_ref, out_ref, upb_ref, head_ref, down_ref, raw_ref,
-    near_ref, far_ref, segment_ref,
+    near_ref, segment_ref,
 ):
     depth = raw_ref.shape[0] - EXTRA
     here = w_ref.shape[0]
     core = lax.axis_index("member")
-    dealt = near_ref.shape[0]
-    lane = iota((8, 1), 0)
+    dealt = near_ref.shape[1]
+    row = iota((8, 1), 0)
     preds = None
     for m in range(here):
         act = gelu2(dot(rows_ref[...], w_ref[m]) + bias_ref[m : m + 1]).astype(BF)
-        on_lane = jnp.where(lane == core * here + m, 0.5 * out_ref[m : m + 1].astype(F32), 0.0).astype(BF)
-        pred = dot_t(act, on_lane)
+        on_row = jnp.where(row == core * here + m, 0.5 * out_ref[m : m + 1].astype(F32), 0.0).astype(BF)
+        pred = dot_t(on_row, act)
         preds = pred if preds is None else preds + pred
-    preds = preds.astype(BF)
-    near_ref[...] = preds[:dealt]
-    far_ref[...] = preds[dealt:]
+    preds = preds.astype(BF).astype(F32)
+    near_ref[...] = preds[:, :dealt]
     head = split3(head_ref[...]).astype(F32)
     head = jnp.concatenate([head, jnp.zeros((LANES - 3, head.shape[1]), F32)], axis=0).astype(BF)
     down = jnp.sum(dot_t(down_ref[...], head).T[:8], axis=0, keepdims=True)
     extra = [split3(x).astype(F32) for x in (down, upb_ref[...], head_ref[...])]
-    extra.append(jnp.zeros((EXTRA - 9, down.shape[1]), F32))
+    members = EXTRA - PREDS
+    far = jnp.concatenate([preds[:members, dealt:], jnp.zeros((members, down.shape[1] - dealt), F32)], axis=1)
+    extra.append(far)
     segment_ref[depth:, :] = jnp.concatenate(extra, axis=0).astype(BF)
 
 
@@ -182,10 +183,10 @@
 
 
 def attend_kernel(
-    members, rows_ref, near_ref, far_ref, place_ref, table_ref, fw0_ref, fw1_ref, q0_ref, q1_ref, *sent_refs
+    members, rows_ref, near_ref, other_ref, place_ref, table_ref, fw0_ref, fw1_ref, q0_ref, q1_ref, *sent_refs
 ):
     core = lax.axis_index("member")
-    total = near_ref.shape[0]
+    total = near_ref.shape[1]
     fwidth = rows_ref.shape[1]
     rows = rows_ref[:total]
     local = q0_ref.shape[2]
@@ -196,7 +197,9 @@
     token = dot(first, fw0_ref[: fwidth // 2]) + dot(second, fw1_ref[: fwidth // 2]) + table_ref[FBIAS : FBIAS + 1, :]
     centered = centre(token)
     tokens = [(centered * inverse_spread(centered) * gain).astype(BF)]
-    preds = near_ref[...].astype(F32) + far_ref[...].astype(F32)
+    first = other_ref.shape[0] - EXTRA + PREDS
+    far = other_ref[first : first + EXTRA - PREDS, :total].astype(F32)
+    preds = (near_ref[...] + jnp.concatenate([far, jnp.zeros((8 - far.shape[0], total), F32)], axis=0)).T
     for m in range(members):
         centered = preds[:, m : m + 1] * table_ref[SCALE + m : SCALE + m + 1, :] + table_ref[SHIFT + m : SHIFT + m + 1, :]
         tokens.append((centered * inverse_spread(centered) * gain).astype(BF))
@@ -399,17 +402,16 @@
         cost_estimate=cost(2 * count * rows * fwidth, 3 * 10**6),
         name="route",
     )(*in_hbm(ins))
-    near, far, segment = pl.pallas_call(
+    near, segment = pl.pallas_call(
         predict_kernel,
-        out_shape=[shape((dealt, 8), BF), shape((dealt, 8), BF), shape(segment.shape, BF)],
+        out_shape=[shape((8, dealt), F32), shape(segment.shape, BF)],
         in_specs=[VMEM] * 8,
-        out_specs=[VMEM] * 3,
-        input_output_aliases={7: 2},
+        out_specs=[VMEM] * 2,
+        input_output_aliases={7: 1},
         compiler_params=params(24),
         cost_estimate=cost(2 * here * count * fwidth * hidden, 3 * 10**6, here * count * hidden),
         name="predict",
     )(mine, member_in, member_bias, member_out, up_bias, owner_heads, down, segment)
-    far = swap(far)
     other_both = swap(own_both)
     next_segment = lax.ppermute(segment, "rows", [(i, i ^ 1) for i in range(n)])
     other_segment = swap(segment)
@@ -434,7 +436,7 @@
         compiler_params=params(24),
         cost_estimate=cost(10**9, 2 * 10**6),
         name="attend",
-    )(mine, near, far, place, table, own_both, other_both, qkv_weight, other_qkv)
+    )(mine, near, other_segment, place, table, own_both, other_both, qkv_weight, other_qkv)
 
     def across(x, k):
         return lax.ppermute(x, "rows", [(i, i ^ (2 * k)) for i in range(n)])

time: 32.7 us -> 32.4 us (level)
  waiting for transfers between devices: 7.66 us -> 7.15 us
    ppermute x6 -> x5, waiting for transfers between devices: 1.62 us -> 1.29 us  [swap(): return lax.ppermute(x, 'member', [(0, 1), (1, 0)])]
    ppermute x6 -> x5, starting transfers between devices: 1.36 us -> 1.18 us  [swap(): return lax.ppermute(x, 'member', [(0, 1), (1, 0)])]
  transfers between devices with their start and end apart: 12 -> 11, of which waited for: 6 -> 5; matrix products, arithmetic and copies ran while one was open for 0% -> 0% of each run, Pallas kernels for 38% -> 38%
where the time goes in v1:
time: 32.4 us; the launch traced here: 32.2 us
  Pallas kernels  13.7 us (42%)
  starting transfers between devices  11 us (34%)
  waiting for transfers between devices  7.15 us (22%)
    ppermute x5, starting transfers between devices, across(): return lax.ppermute(x, 'rows', [(i, i ^ 2 * k) for i in range(n)])  7.04 us
    ppermute x5, waiting for transfers between devices, across(): return lax.ppermute(x, 'rows', [(i, i ^ 2 * k) for i in range(n)])  5.86 us
    pallas_call x3, Pallas kernels, ensemble(): pl.pallas_call(functools.partial(ensemble_kernel, first, number, tile), o...  4.66 us
    ppermute x1, starting transfers between devices, per_device(): next_segment = lax.ppermute(segment, 'rows', [(i, i ^ 1) for i in range(n)])  2.76 us
    pallas_call x1, Pallas kernels, per_device(): pl.pallas_call(functools.partial(attend_kernel, members), out_shape=[shap...  2.12 us
    pallas_call x1, Pallas kernels, per_device(): pl.pallas_call(functools.partial(route_kernel, n, half, relative), out_sh...  1.91 us
    pallas_call x1, Pallas kernels, per_device(): pl.pallas_call(predict_kernel, out_shape=[shape((8, dealt), F32), shape(s...  1.34 us
    ppermute x5, waiting for transfers between devices, swap(): return lax.ppermute(x, 'member', [(0, 1), (1, 0)])  1.29 us
  transfers between devices with their start and end apart: 11, of which 5 were waited for; matrix products, arithmetic and copies ran while one was open for 0% of the time, Pallas kernels for 38%

profile of v1, /device:TPU:0, one launch (start us, length us, event | category | flops | bytes accessed | tf_op | source)
XLA Modules:
  0.0 32.2 jit_solution(1036013583750081455)
XLA Ops:
  0.0 0.5 %collective-permute-start = (bf16[3,512,256]{2,1,0:T(8,128)(2,1)}, bf16[3,512,256]{2,1,0:T(8,128)(2,1)S(1)}, u32[]{:S(2)}, u32[]{:S(2)}) collective-permute-start(bf16[3,512,256]{2,1,0:T(8,128)(2,1)} %q0_ref.3), channel_id=1, source_target_pairs={{0,1},{1,0},{2,3},{3,2},{4,5},{5,4},{6,7},{7,6},{8,9},{9,8},{10,11... | collective-permute-start | bytes 2359304 | tf_op jit(solution)/shard_map/ppermute | solution.py:380
  0.5 1.9 %route.1 = (s32[8,256]{1,0:T(8,128)S(1)}, bf16[256,512]{1,0:T(8,128)(2,1)S(1)}, bf16[512,512]{1,0:T(8,128)(2,1)S(1)}, bf16[528,512]{1,0:T(8,128)(2,1)S(1)}, bf16[512,512]{1,0:T(8,128)(2,1)S(1)}) custom-call(s32[1,256]{1,0:T(1,128)} %esc_hbm.1, s32[1,256]{1,0:T(1,128)} %bitcast.10, bf16[1024,512]{1,0:T(8,128)(2,1)} %feat_ref.5, ...), custom_call_target="tpu_custom_call" | custom-call | flops 268435456 | bytes 3000000 | tf_op jit(solution)/shard_map/route/pallas_call | solution.py:393
  2.6 1.3 %predict.1 = (f32[8,128]{1,0:T(8,128)S(1)}, bf16[528,512]{1,0:T(8,128)(2,1)S(1)}) custom-call(bf16[256,512]{1,0:T(8,128)(2,1)S(1)} %get-tuple-element.31.rows_ref, bf16[2,512,1024]{2,1,0:T(8,128)(2,1)S(1)} %copy-done, f32[2,1024]{1,0:T(2,128)S(1)} %copy-done.3, bf16[2,1024]{1,0:T(2,128)(2,1)S(1)} %copy-done.4, ...), custom_call_target="tpu_custom_call", output_to_operand_aliasing={{1}: (7, {})} | custom-call | flops 536870912 | bytes 3000000 | tf_op jit(solution)/shard_map/predict/pallas_call | solution.py:405
  3.9 0.3 collective-permute-start.1
  4.5 2.8 %collective-permute-start.7 = (bf16[528,512]{1,0:T(8,128)(2,1)S(1)}, bf16[528,512]{1,0:T(8,128)(2,1)S(1)}, u32[]{:S(2)}, u32[]{:S(2)}) collective-permute-start(bf16[528,512]{1,0:T(8,128)(2,1)S(1)} %get-tuple-element.35.refs_3_), channel_id=1, source_target_pairs={{0,2},{2,0},{4,6},{6,4},{8,10},{10,8},{12,14},{14,12},{1,3},{3,1},... | collective-permute-start | bytes 1622024 | tf_op jit(solution)/shard_map/ppermute | solution.py:416
  7.3 0.7 %constants.1 = (f32[40,512]{1,0:T(8,128)S(1)}, s32[256,3]{1,0:T(8,128)S(1)}, s32[1,128]{1,0:T(1,128)S(1)}) custom-call(f32[1,512]{1,0:T(1,128)S(1)} %bitcast.6, f32[1,512]{1,0:T(1,128)S(1)} %bitcast.7, f32[4,512]{1,0:T(4,128)S(1)} %copy-done.5, f32[4,512]{1,0:T(4,128)S(1)} %copy-done.6, f32[1,512]{1,0:T(1,128)S(1)} %bitcast.8, f32[1,512]{1,0:T(1,128)S(1)} %bitcast.9, ...), custom_call_target="tpu_custom_call" | custom-call | flops 100000000 | bytes 2000000 | tf_op jit(solution)/shard_map/constants/pallas_call | solution.py:420
  8.1 2.1 %attend.1 = (bf16[64,512]{1,0:T(8,128)(2,1)S(1)}, bf16[64,512]{1,0:T(8,128)(2,1)S(1)}, bf16[64,512]{1,0:T(8,128)(2,1)S(1)}, bf16[64,512]{1,0:T(8,128)(2,1)S(1)}) custom-call(bf16[256,512]{1,0:T(8,128)(2,1)S(1)} %get-tuple-element.31.rows_ref, f32[8,128]{1,0:T(8,128)S(1)} %get-tuple-element.34.near_ref, ...), custom_call_target="tpu_custom_call" | custom-call | flops 1000000000 | bytes 2000000 | tf_op jit(solution)/shard_map/attend/pallas_call | solution.py:431
  10.2 3.7 %collective-permute-start.3 = (bf16[64,512]{1,0:T(8,128)(2,1)S(1)}, bf16[64,512]{1,0:T(8,128)(2,1)S(1)}, u32[]{:S(2)}, u32[]{:S(2)}) collective-permute-start(bf16[64,512]{1,0:T(8,128)(2,1)S(1)} %get-tuple-element.39), channel_id=1, source_target_pairs={{0,12},{2,14},{4,8},{6,10},{8,4},{10,6},{12,0},{14,2},{1,13},{3,15... | collective-permute-start | bytes 196616 | tf_op jit(solution)/shard_map/ppermute | solution.py:442
  13.9 0.8 %collective-permute-start.5 = (bf16[64,512]{1,0:T(8,128)(2,1)S(1)}, bf16[64,512]{1,0:T(8,128)(2,1)S(1)}, u32[]{:S(2)}, u32[]{:S(2)}) collective-permute-start(bf16[64,512]{1,0:T(8,128)(2,1)S(1)} %get-tuple-element.41), channel_id=1, source_target_pairs={{0,4},{2,6},{4,0},{6,2},{8,12},{10,14},{12,8},{14,10},{1,5},{3,7},... | collective-permute-start | bytes 196616 | tf_op jit(solution)/shard_map/ppermute | solution.py:442
  14.6 2.4 %ensemble.3 = (f32[4,128]{1,0:T(4,128)S(1)}, f32[40,512]{1,0:T(8,128)S(1)}, bf16[512,512]{1,0:T(8,128)(2,1)S(1)}, bf16[512,512]{1,0:T(8,128)(2,1)S(1)}, bf16[528...) custom-call(bf16[1024,512]{1,0:T(8,128)(2,1)S(1)} %copy-done.1, bf16[2,512,1024]{2,1,0:T(8,128)(2,1)S(1)} %copy-done, ...), custom_call_target="tpu_custom_call" | custom-call | flops 1073741824 | bytes 1000000 | tf_op jit(solution)/shard_map/ensemble/pallas_call | solution.py:458
  17.0 2.6 %collective-permute-done.4.refs_1_ = bf16[64,512]{1,0:T(8,128)(2,1)S(1)} collective-permute-done((bf16[64,512]{1,0:T(8,128)(2,1)S(1)}, bf16[64,512]{1,0:T(8,128)(2,1)S(1)}, u32[]{:S(2)}, u32[]{:S(2)}) %collective-permute-start.4) | collective-permute-done | bytes 65568 | tf_op jit(solution)/shard_map/ppermute | solution.py:442
  19.6 0.4 %arrive.1 = (f32[128,512]{1,0:T(8,128)S(1)}, bf16[128,512]{1,0:T(8,128)(2,1)S(1)}) custom-call(bf16[64,512]{1,0:T(8,128)(2,1)S(1)} %collective-permute-done.3.refs_0_, bf16[64,512]{1,0:T(8,128)(2,1)S(1)} %collective-permute-done.4.refs_1_, bf16[64,512]{1,0:T(8,128)(2,1)S(1)} %collective-permute-done.5.refs_2_, ...), custom_call_target="tpu_custom_call" | custom-call | flops 200000000 | bytes 2000000 | tf_op jit(solution)/shard_map/arrive/pallas_call | solution.py:474
  20.1 0.8 %near_score.1.near_ref = f32[128,1]{1,0:T(8,128)S(1)} custom-call(bf16[64,512]{1,0:T(8,128)(2,1)S(1)} %collective-permute-done.3.refs_0_, bf16[64,512]{1,0:T(8,128)(2,1)S(1)} %collective-permute-done.4.refs_1_, bf16[64,512]{1,0:T(8,128)(2,1)S(1)} %collective-permute-done.5.refs_2_, bf16[64,512]{1,0:T(8,128)(2,1)S(1)} %get-tuple-element.42.after_ref.refs_3_, ...), custom_call_target="tpu_custom_call" | custom-call | flops 500000000 | bytes 2000000 | tf_op jit(solution)/shard_map/near_score/pallas_call | solution.py:484
  20.9 0.6 %collective-permute-done.6.other_ref = bf16[128,512]{1,0:T(8,128)(2,1)S(1)} collective-permute-done((bf16[128,512]{1,0:T(8,128)(2,1)S(1)}, bf16[128,512]{1,0:T(8,128)(2,1)S(1)}, u32[]{:S(2)}, u32[]{:S(2)}) %collective-permute-start.6) | collective-permute-done | bytes 131104 | tf_op jit(solution)/shard_map/ppermute | solution.py:380
  21.4 0.4 %far_score.1.after_ref = f32[4,128]{1,0:T(4,128)S(1)} custom-call(f32[128,1]{1,0:T(8,128)S(1)} %near_score.1.near_ref, f32[128,512]{1,0:T(8,128)S(1)} %get-tuple-element.48.state_ref, bf16[128,512]{1,0:T(8,128)(2,1)S(1)} %get-tuple-element.49.mine_ref, bf16[128,512]{1,0:T(8,128)(2,1)S(1)} %collective-permute-done.6.other_ref, ...), custom_call_target="tpu_custom_call" | custom-call | flops 200000000 | bytes 1000000 | tf_op jit(solution)/shard_map/far_score/pallas_call | solution.py:493
  21.9 1.1 %collective-permute-start.8 = (f32[4,128]{1,0:T(4,128)S(1)}, f32[4,128]{1,0:T(4,128)S(1)}, u32[]{:S(2)}, u32[]{:S(2)}) collective-permute-start(f32[4,128]{1,0:T(4,128)S(1)} %far_score.1.after_ref), channel_id=1, source_target_pairs={{0,4},{2,6},{4,0},{6,2},{8,12},{10,14},{12,8},{14,10},{1,5},{3,7},... | collective-permute-start | bytes 6152 | tf_op jit(solution)/shard_map/ppermute | solution.py:442
  23.0 1.1 %ensemble.4.after_ref = f32[2,128]{1,0:T(2,128)S(1)} custom-call(bf16[1024,512]{1,0:T(8,128)(2,1)S(1)} %copy-done.1, bf16[2,512,1024]{2,1,0:T(8,128)(2,1)S(1)} %copy-done, f32[2,1024]{1,0:T(2,128)S(1)} %copy-done.3, bf16[2,1024]{1,0:T(2,128)(2,1)S(1)} %copy-done.4, f32[4,128]{1,0:T(4,128)S(1)} %far_score.1.after_ref), custom_call_target="tpu_custom_call" | custom-call | flops 536870912 | bytes 1000000 | tf_op jit(solution)/shard_map/ensemble/pallas_call | solution.py:458
  24.2 1.4 %collective-permute-done.8 = f32[4,128]{1,0:T(4,128)S(1)} collective-permute-done((f32[4,128]{1,0:T(4,128)S(1)}, f32[4,128]{1,0:T(4,128)S(1)}, u32[]{:S(2)}, u32[]{:S(2)}) %collective-permute-start.8) | collective-permute-done | bytes 2080 | tf_op jit(solution)/shard_map/ppermute | solution.py:442
  25.5 1.4 %collective-permute-start.9 = (f32[8,128]{1,0:T(8,128)S(1)}, f32[8,128]{1,0:T(8,128)S(1)}, u32[]{:S(2)}, u32[]{:S(2)}) collective-permute-start(f32[8,128]{1,0:T(8,128)S(1)} %pad_maximum_fusion), channel_id=1, source_target_pairs={{0,8},{2,10},{4,12},{6,14},{8,0},{10,2},{12,4},{14,6},{1,9},{3,11}... | collective-permute-start | bytes 12296 | tf_op jit(solution)/shard_map/ppermute | solution.py:442
  27.0 1.1 %ensemble.5 = f32[2,128]{1,0:T(2,128)S(1)} custom-call(bf16[1024,512]{1,0:T(8,128)(2,1)S(1)} %copy-done.1, bf16[2,512,1024]{2,1,0:T(8,128)(2,1)S(1)} %copy-done, f32[2,1024]{1,0:T(2,128)S(1)} %copy-done.3, bf16[2,1024]{1,0:T(2,128)(2,1)S(1)} %copy-done.4, f32[4,128]{1,0:T(4,128)S(1)} %far_score.1.after_ref), custom_call_target="tpu_custom_call" | custom-call | flops 536870912 | bytes 1000000 | tf_op jit(solution)/shard_map/ensemble/pallas_call | solution.py:458
  28.1 1.9 %collective-permute-done.9 = f32[8,128]{1,0:T(8,128)S(1)} collective-permute-done((f32[8,128]{1,0:T(8,128)S(1)}, f32[8,128]{1,0:T(8,128)S(1)}, u32[]{:S(2)}, u32[]{:S(2)}) %collective-permute-start.9) | collective-permute-done | bytes 4128 | tf_op jit(solution)/shard_map/ppermute | solution.py:442
  30.1 0.4 %expand.1 = (bf16[96,1024]{1,0:T(8,128)(2,1)S(1)}, s32[1,1024]{1,0:T(1,128)S(1)}) custom-call(s32[256,3]{1,0:T(8,128)S(1)} %get-tuple-element.30.where_ref, f32[2,128]{1,0:T(2,128)S(1)} %ensemble.4.after_ref), custom_call_target="tpu_custom_call" | custom-call | flops 100000000 | bytes 1000000 | tf_op jit(solution)/shard_map/expand/pallas_call | solution.py:515
  30.6 0.7 %collective-permute-done.10.far_ref = f32[24,128]{1,0:T(8,128)S(1)} collective-permute-done((f32[24,128]{1,0:T(8,128)S(1)}, f32[24,128]{1,0:T(8,128)S(1)}, u32[]{:S(2)}, u32[]{:S(2)}) %collective-permute-start.10) | collective-permute-done | bytes 12320 | tf_op jit(solution)/shard_map/ppermute | solution.py:380
  31.3 0.9 %finish.1 = f32[1,1024]{1,0:T(1,128)} custom-call(bf16[96,1024]{1,0:T(8,128)(2,1)S(1)} %get-tuple-element.50.line_ref, s32[1,1024]{1,0:T(1,128)S(1)} %get-tuple-element.51.lane_ref, f32[24,128]{1,0:T(8,128)S(1)} %concatenate.8.near_ref, f32[24,128]{1,0:T(8,128)S(1)} %collective-permute-done.10.far_ref), custom_call_target="tpu_custom_call" | custom-call | flops 1000000 | bytes 1000000 | tf_op jit(solution)/shard_map/finish/pallas_call | solution.py:525
  (38 shorter events, 0.5 us)
Async XLA Ops:
  0.0 2.6 %copy-start = (bf16[2,512,1024]{2,1,0:T(8,128)(2,1)S(1)}, bf16[2,512,1024]{2,1,0:T(8,128)(2,1)}, u32[]{:S(2)}) copy-start(bf16[2,512,1024]{2,1,0:T(8,128)(2,1)} %w_ref.7) | copy-start | bytes 6291460
  0.0 2.6 %copy-start.3 = (f32[2,1024]{1,0:T(2,128)S(1)}, f32[2,1024]{1,0:T(2,128)}, u32[]{:S(2)}) copy-start(f32[2,1024]{1,0:T(2,128)} %bias_ref.7) | copy-start | bytes 24580
  0.0 2.6 %copy-start.4 = (bf16[2,1024]{1,0:T(2,128)(2,1)S(1)}, bf16[2,1024]{1,0:T(2,128)(2,1)}, u32[]{:S(2)}) copy-start(bf16[2,1024]{1,0:T(2,128)(2,1)} %out_ref.7) | copy-start | bytes 12292
  0.0 2.6 %copy-start.11 = (f32[1,512]{1,0:T(1,128)S(1)}, f32[1,512]{1,0:T(1,128)}, u32[]{:S(2)}) copy-start(f32[1,512]{1,0:T(1,128)} %upb_ref.1) | copy-start | bytes 6148
  0.0 2.6 %copy-start.12 = (f32[1,512]{1,0:T(1,128)S(1)}, f32[1,512]{1,0:T(1,128)}, u32[]{:S(2)}) copy-start(f32[1,512]{1,0:T(1,128)} %head_ref.1) | copy-start | bytes 6148
  0.0 7.2 %collective-permute-start = (bf16[3,512,256]{2,1,0:T(8,128)(2,1)}, bf16[3,512,256]{2,1,0:T(8,128)(2,1)S(1)}, u32[]{:S(2)}, u32[]{:S(2)}) collective-permute-start(bf16[3,512,256]{2,1,0:T(8,128)(2,1)} %q0_ref.3), channel_id=1, source_target_pairs={{0,1},{1,0},{2,3},{3,2},{4,5},{5,4},{6,7},{7,6},{8,9},{9,8},{10,11... | collective-permute-start | bytes 2359304 | tf_op jit(solution)/shard_map/ppermute | solution.py:380
  2.5 4.8 %copy-start.2 = (bf16[3,512,256]{2,1,0:T(8,128)(2,1)S(1)}, bf16[3,512,256]{2,1,0:T(8,128)(2,1)}, u32[]{:S(2)}) copy-start(bf16[3,512,256]{2,1,0:T(8,128)(2,1)} %q0_ref.3) | copy-start | bytes 2359300
  2.5 4.7 %copy-start.5 = (f32[4,512]{1,0:T(4,128)S(1)}, f32[4,512]{1,0:T(4,128)}, u32[]{:S(2)}) copy-start(f32[4,512]{1,0:T(4,128)} %scale_ref.1) | copy-start | bytes 24580
  2.5 4.7 %copy-start.6 = (f32[4,512]{1,0:T(4,128)S(1)}, f32[4,512]{1,0:T(4,128)}, u32[]{:S(2)}) copy-start(f32[4,512]{1,0:T(4,128)} %shift_ref.1) | copy-start | bytes 24580
  2.5 4.7 %copy-start.7 = (f32[512]{0:T(512)S(1)}, f32[512]{0:T(512)}, u32[]{:S(2)}) copy-start(f32[512]{0:T(512)} %param.29) | copy-start | bytes 6148
  2.5 4.7 %copy-start.8 = (f32[512]{0:T(512)S(1)}, f32[512]{0:T(512)}, u32[]{:S(2)}) copy-start(f32[512]{0:T(512)} %param.30) | copy-start | bytes 6148
  2.5 4.7 %copy-start.9 = (f32[512]{0:T(512)S(1)}, f32[512]{0:T(512)}, u32[]{:S(2)}) copy-start(f32[512]{0:T(512)} %param.26) | copy-start | bytes 6148
  2.5 4.7 %copy-start.10 = (f32[512]{0:T(512)S(1)}, f32[512]{0:T(512)}, u32[]{:S(2)}) copy-start(f32[512]{0:T(512)} %param.33) | copy-start | bytes 6148
  3.9 4.1 %collective-permute-start.1 = (bf16[528,512]{1,0:T(8,128)(2,1)S(1)}, bf16[528,512]{1,0:T(8,128)(2,1)S(1)}, u32[]{:S(2)}, u32[]{:S(2)}) collective-permute-start(bf16[528,512]{1,0:T(8,128)(2,1)S(1)} %get-tuple-element.35.refs_3_), channel_id=1, source_target_pairs={{0,1},{1,0},{2,3},{3,2},{4,5},{5,4},{6,7},{7,6},{8,9},{9,8},{10,11... | collective-permute-start | bytes 1622024 | tf_op jit(solution)/shard_map/ppermute | solution.py:380
  4.2 3.8 %collective-permute-start.2 = (bf16[512,512]{1,0:T(8,128)(2,1)S(1)}, bf16[512,512]{1,0:T(8,128)(2,1)S(1)}, u32[]{:S(2)}, u32[]{:S(2)}) collective-permute-start(bf16[512,512]{1,0:T(8,128)(2,1)S(1)} %get-tuple-element.38.fw0_ref.refs_1_), channel_id=1, source_target_pairs={{0,1},{1,0},{2,3},{3,2},{4,5},{5,4},{6,7},{7,6},{8,9},{9,8},{10,11... | collective-permute-start | bytes 1572872 | tf_op jit(solution)/shard_map/ppermute | solution.py:380
  4.5 16.4 %collective-permute-start.7 = (bf16[528,512]{1,0:T(8,128)(2,1)S(1)}, bf16[528,512]{1,0:T(8,128)(2,1)S(1)}, u32[]{:S(2)}, u32[]{:S(2)}) collective-permute-start(bf16[528,512]{1,0:T(8,128)(2,1)S(1)} %get-tuple-element.35.refs_3_), channel_id=1, source_target_pairs={{0,2},{2,0},{4,6},{6,4},{8,10},{10,8},{12,14},{14,12},{1,3},{3,1},... | collective-permute-start | bytes 1622024 | tf_op jit(solution)/shard_map/ppermute | solution.py:416
  8.0 6.6 %copy-start.1 = (bf16[1024,512]{1,0:T(8,128)(2,1)S(1)}, bf16[1024,512]{1,0:T(8,128)(2,1)}, u32[]{:S(2)}) copy-start(bf16[1024,512]{1,0:T(8,128)(2,1)} %feat_ref.5) | copy-start | bytes 3145732
  10.2 6.8 %collective-permute-start.3 = (bf16[64,512]{1,0:T(8,128)(2,1)S(1)}, bf16[64,512]{1,0:T(8,128)(2,1)S(1)}, u32[]{:S(2)}, u32[]{:S(2)}) collective-permute-start(bf16[64,512]{1,0:T(8,128)(2,1)S(1)} %get-tuple-element.39), channel_id=1, source_target_pairs={{0,12},{2,14},{4,8},{6,10},{8,4},{10,6},{12,0},{14,2},{1,13},{3,15... | collective-permute-start | bytes 196616 | tf_op jit(solution)/shard_map/ppermute | solution.py:442
  13.9 5.7 %collective-permute-start.4 = (bf16[64,512]{1,0:T(8,128)(2,1)S(1)}, bf16[64,512]{1,0:T(8,128)(2,1)S(1)}, u32[]{:S(2)}, u32[]{:S(2)}) collective-permute-start(bf16[64,512]{1,0:T(8,128)(2,1)S(1)} %get-tuple-element.40), channel_id=1, source_target_pairs={{0,8},{2,10},{4,12},{6,14},{8,0},{10,2},{12,4},{14,6},{1,9},{3,11}... | collective-permute-start | bytes 196616 | tf_op jit(solution)/shard_map/ppermute | solution.py:442
  13.9 5.7 %collective-permute-start.5 = (bf16[64,512]{1,0:T(8,128)(2,1)S(1)}, bf16[64,512]{1,0:T(8,128)(2,1)S(1)}, u32[]{:S(2)}, u32[]{:S(2)}) collective-permute-start(bf16[64,512]{1,0:T(8,128)(2,1)S(1)} %get-tuple-element.41), channel_id=1, source_target_pairs={{0,4},{2,6},{4,0},{6,2},{8,12},{10,14},{12,8},{14,10},{1,5},{3,7},... | collective-permute-start | bytes 196616 | tf_op jit(solution)/shard_map/ppermute | solution.py:442
  20.0 1.4 %collective-permute-start.6 = (bf16[128,512]{1,0:T(8,128)(2,1)S(1)}, bf16[128,512]{1,0:T(8,128)(2,1)S(1)}, u32[]{:S(2)}, u32[]{:S(2)}) collective-permute-start(bf16[128,512]{1,0:T(8,128)(2,1)S(1)} %get-tuple-element.49.mine_ref), channel_id=1, source_target_pairs={{0,1},{1,0},{2,3},{3,2},{4,5},{5,4},{6,7},{7,6},{8,9},{9,8},{10,11... | collective-permute-start | bytes 393224 | tf_op jit(solution)/shard_map/ppermute | solution.py:380
  21.9 3.7 %collective-permute-start.8 = (f32[4,128]{1,0:T(4,128)S(1)}, f32[4,128]{1,0:T(4,128)S(1)}, u32[]{:S(2)}, u32[]{:S(2)}) collective-permute-start(f32[4,128]{1,0:T(4,128)S(1)} %far_score.1.after_ref), channel_id=1, source_target_pairs={{0,4},{2,6},{4,0},{6,2},{8,12},{10,14},{12,8},{14,10},{1,5},{3,7},... | collective-permute-start | bytes 6152 | tf_op jit(solution)/shard_map/ppermute | solution.py:442
  25.5 4.5 %collective-permute-start.9 = (f32[8,128]{1,0:T(8,128)S(1)}, f32[8,128]{1,0:T(8,128)S(1)}, u32[]{:S(2)}, u32[]{:S(2)}) collective-permute-start(f32[8,128]{1,0:T(8,128)S(1)} %pad_maximum_fusion), channel_id=1, source_target_pairs={{0,8},{2,10},{4,12},{6,14},{8,0},{10,2},{12,4},{14,6},{1,9},{3,11}... | collective-permute-start | bytes 12296 | tf_op jit(solution)/shard_map/ppermute | solution.py:442
  30.1 1.2 %collective-permute-start.10 = (f32[24,128]{1,0:T(8,128)S(1)}, f32[24,128]{1,0:T(8,128)S(1)}, u32[]{:S(2)}, u32[]{:S(2)}) collective-permute-start(f32[24,128]{1,0:T(8,128)S(1)} %concatenate.8.near_ref), channel_id=1, source_target_pairs={{0,1},{1,0},{2,3},{3,2},{4,5},{5,4},{6,7},{7,6},{8,9},{9,8},{10,11... | collective-permute-start | bytes 36872 | tf_op jit(solution)/shard_map/ppermute | solution.py:380

commit v2 on v1

--- a/solution.py
+++ b/solution.py
@@ -200,9 +200,18 @@
     first = other_ref.shape[0] - EXTRA + PREDS
     far = other_ref[first : first + EXTRA - PREDS, :total].astype(F32)
     preds = (near_ref[...] + jnp.concatenate([far, jnp.zeros((8 - far.shape[0], total), F32)], axis=0)).T
+    scale, shift = table_ref[SCALE : SCALE + 8, :], table_ref[SHIFT : SHIFT + 8, :]
+    square = jnp.mean(scale * scale, axis=-1, keepdims=True)
+    ratio = jnp.mean(scale * shift, axis=-1, keepdims=True) / jnp.maximum(square, 1e-30)
+    rest = shift - ratio * scale
+    rest = jnp.mean(rest * rest, axis=-1, keepdims=True) + EPS
+    scale, shift = scale * gain, shift * gain
     for m in range(members):
-        centered = preds[:, m : m + 1] * table_ref[SCALE + m : SCALE + m + 1, :] + table_ref[SHIFT + m : SHIFT + m + 1, :]
-        tokens.append((centered * inverse_spread(centered) * gain).astype(BF))
+        at = slice(m, m + 1)
+        pred = preds[:, at]
+        moved = pred + ratio[at]
+        inverse = lax.rsqrt(square[at] * moved * moved + rest[at])
+        tokens.append(((pred * inverse) * scale[at] + inverse * shift[at]).astype(BF))
     normed = jnp.concatenate(tokens, axis=0)
     count = len(tokens)
 

time: 32.4 us -> 32.3 us (level)
  no operation moved by 1% of the time
where the time goes in v2:
time: 32.3 us; the launch traced here: 32.2 us
  Pallas kernels  13.7 us (42%)
  starting transfers between devices  11 us (34%)
  waiting for transfers between devices  7.14 us (22%)
    ppermute x5, starting transfers between devices, across(): return lax.ppermute(x, 'rows', [(i, i ^ 2 * k) for i in range(n)])  7.04 us
    ppermute x5, waiting for transfers between devices, across(): return lax.ppermute(x, 'rows', [(i, i ^ 2 * k) for i in range(n)])  5.85 us
    pallas_call x3, Pallas kernels, ensemble(): pl.pallas_call(functools.partial(ensemble_kernel, first, number, tile), o...  4.67 us
    ppermute x1, starting transfers between devices, per_device(): next_segment = lax.ppermute(segment, 'rows', [(i, i ^ 1) for i in range(n)])  2.76 us
    pallas_call x1, Pallas kernels, per_device(): pl.pallas_call(functools.partial(attend_kernel, members), out_shape=[shap...  2.04 us
    pallas_call x1, Pallas kernels, per_device(): pl.pallas_call(functools.partial(route_kernel, n, half, relative), out_sh...  1.91 us
    pallas_call x1, Pallas kernels, per_device(): pl.pallas_call(predict_kernel, out_shape=[shape((8, dealt), F32), shape(s...  1.34 us
    ppermute x5, waiting for transfers between devices, swap(): return lax.ppermute(x, 'member', [(0, 1), (1, 0)])  1.29 us
  transfers between devices with their start and end apart: 11, of which 5 were waited for; matrix products, arithmetic and copies ran while one was open for 0% of the time, Pallas kernels for 38%

profile of v2, /device:TPU:0, one launch (start us, length us, event | category | flops | bytes accessed | tf_op | source)
XLA Modules:
  0.0 32.2 jit_solution(10496826754682561591)
XLA Ops:
  0.0 0.5 %collective-permute-start = (bf16[3,512,256]{2,1,0:T(8,128)(2,1)}, bf16[3,512,256]{2,1,0:T(8,128)(2,1)S(1)}, u32[]{:S(2)}, u32[]{:S(2)}) collective-permute-start(bf16[3,512,256]{2,1,0:T(8,128)(2,1)} %q0_ref.3), channel_id=1, source_target_pairs={{0,1},{1,0},{2,3},{3,2},{4,5},{5,4},{6,7},{7,6},{8,9},{9,8},{10,11... | collective-permute-start | bytes 2359304 | tf_op jit(solution)/shard_map/ppermute | solution.py:389
  0.5 1.9 %route.1 = (s32[8,256]{1,0:T(8,128)S(1)}, bf16[256,512]{1,0:T(8,128)(2,1)S(1)}, bf16[512,512]{1,0:T(8,128)(2,1)S(1)}, bf16[528,512]{1,0:T(8,128)(2,1)S(1)}, bf16[512,512]{1,0:T(8,128)(2,1)S(1)}) custom-call(s32[1,256]{1,0:T(1,128)} %esc_hbm.1, s32[1,256]{1,0:T(1,128)} %bitcast.10, bf16[1024,512]{1,0:T(8,128)(2,1)} %feat_ref.5, ...), custom_call_target="tpu_custom_call" | custom-call | flops 268435456 | bytes 3000000 | tf_op jit(solution)/shard_map/route/pallas_call | solution.py:402
  2.6 1.3 %predict.1 = (f32[8,128]{1,0:T(8,128)S(1)}, bf16[528,512]{1,0:T(8,128)(2,1)S(1)}) custom-call(bf16[256,512]{1,0:T(8,128)(2,1)S(1)} %get-tuple-element.31.rows_ref, bf16[2,512,1024]{2,1,0:T(8,128)(2,1)S(1)} %copy-done, f32[2,1024]{1,0:T(2,128)S(1)} %copy-done.3, bf16[2,1024]{1,0:T(2,128)(2,1)S(1)} %copy-done.4, ...), custom_call_target="tpu_custom_call", output_to_operand_aliasing={{1}: (7, {})} | custom-call | flops 536870912 | bytes 3000000 | tf_op jit(solution)/shard_map/predict/pallas_call | solution.py:414
  3.9 0.3 collective-permute-start.1
  4.5 2.8 %collective-permute-start.7 = (bf16[528,512]{1,0:T(8,128)(2,1)S(1)}, bf16[528,512]{1,0:T(8,128)(2,1)S(1)}, u32[]{:S(2)}, u32[]{:S(2)}) collective-permute-start(bf16[528,512]{1,0:T(8,128)(2,1)S(1)} %get-tuple-element.35.refs_3_), channel_id=1, source_target_pairs={{0,2},{2,0},{4,6},{6,4},{8,10},{10,8},{12,14},{14,12},{1,3},{3,1},... | collective-permute-start | bytes 1622024 | tf_op jit(solution)/shard_map/ppermute | solution.py:425
  7.3 0.7 %constants.1 = (f32[40,512]{1,0:T(8,128)S(1)}, s32[256,3]{1,0:T(8,128)S(1)}, s32[1,128]{1,0:T(1,128)S(1)}) custom-call(f32[1,512]{1,0:T(1,128)S(1)} %bitcast.6, f32[1,512]{1,0:T(1,128)S(1)} %bitcast.7, f32[4,512]{1,0:T(4,128)S(1)} %copy-done.5, f32[4,512]{1,0:T(4,128)S(1)} %copy-done.6, f32[1,512]{1,0:T(1,128)S(1)} %bitcast.8, f32[1,512]{1,0:T(1,128)S(1)} %bitcast.9, ...), custom_call_target="tpu_custom_call" | custom-call | flops 100000000 | bytes 2000000 | tf_op jit(solution)/shard_map/constants/pallas_call | solution.py:429
  8.1 2.0 %attend.1 = (bf16[64,512]{1,0:T(8,128)(2,1)S(1)}, bf16[64,512]{1,0:T(8,128)(2,1)S(1)}, bf16[64,512]{1,0:T(8,128)(2,1)S(1)}, bf16[64,512]{1,0:T(8,128)(2,1)S(1)}) custom-call(bf16[256,512]{1,0:T(8,128)(2,1)S(1)} %get-tuple-element.31.rows_ref, f32[8,128]{1,0:T(8,128)S(1)} %get-tuple-element.34.near_ref, ...), custom_call_target="tpu_custom_call" | custom-call | flops 1000000000 | bytes 2000000 | tf_op jit(solution)/shard_map/attend/pallas_call | solution.py:440
  10.1 3.7 %collective-permute-start.3 = (bf16[64,512]{1,0:T(8,128)(2,1)S(1)}, bf16[64,512]{1,0:T(8,128)(2,1)S(1)}, u32[]{:S(2)}, u32[]{:S(2)}) collective-permute-start(bf16[64,512]{1,0:T(8,128)(2,1)S(1)} %get-tuple-element.39), channel_id=1, source_target_pairs={{0,12},{2,14},{4,8},{6,10},{8,4},{10,6},{12,0},{14,2},{1,13},{3,15... | collective-permute-start | bytes 196616 | tf_op jit(solution)/shard_map/ppermute | solution.py:451
  13.8 0.8 %collective-permute-start.5 = (bf16[64,512]{1,0:T(8,128)(2,1)S(1)}, bf16[64,512]{1,0:T(8,128)(2,1)S(1)}, u32[]{:S(2)}, u32[]{:S(2)}) collective-permute-start(bf16[64,512]{1,0:T(8,128)(2,1)S(1)} %get-tuple-element.41), channel_id=1, source_target_pairs={{0,4},{2,6},{4,0},{6,2},{8,12},{10,14},{12,8},{14,10},{1,5},{3,7},... | collective-permute-start | bytes 196616 | tf_op jit(solution)/shard_map/ppermute | solution.py:451
  14.6 2.4 %ensemble.3 = (f32[4,128]{1,0:T(4,128)S(1)}, f32[40,512]{1,0:T(8,128)S(1)}, bf16[512,512]{1,0:T(8,128)(2,1)S(1)}, bf16[512,512]{1,0:T(8,128)(2,1)S(1)}, bf16[528...) custom-call(bf16[1024,512]{1,0:T(8,128)(2,1)S(1)} %copy-done.1, bf16[2,512,1024]{2,1,0:T(8,128)(2,1)S(1)} %copy-done, ...), custom_call_target="tpu_custom_call" | custom-call | flops 1073741824 | bytes 1000000 | tf_op jit(solution)/shard_map/ensemble/pallas_call | solution.py:467
  17.0 2.6 %collective-permute-done.4.refs_1_ = bf16[64,512]{1,0:T(8,128)(2,1)S(1)} collective-permute-done((bf16[64,512]{1,0:T(8,128)(2,1)S(1)}, bf16[64,512]{1,0:T(8,128)(2,1)S(1)}, u32[]{:S(2)}, u32[]{:S(2)}) %collective-permute-start.4) | collective-permute-done | bytes 65568 | tf_op jit(solution)/shard_map/ppermute | solution.py:451
  19.5 0.4 %arrive.1 = (f32[128,512]{1,0:T(8,128)S(1)}, bf16[128,512]{1,0:T(8,128)(2,1)S(1)}) custom-call(bf16[64,512]{1,0:T(8,128)(2,1)S(1)} %collective-permute-done.3.refs_0_, bf16[64,512]{1,0:T(8,128)(2,1)S(1)} %collective-permute-done.4.refs_1_, bf16[64,512]{1,0:T(8,128)(2,1)S(1)} %collective-permute-done.5.refs_2_, ...), custom_call_target="tpu_custom_call" | custom-call | flops 200000000 | bytes 2000000 | tf_op jit(solution)/shard_map/arrive/pallas_call | solution.py:483
  20.0 0.8 %near_score.1.near_ref = f32[128,1]{1,0:T(8,128)S(1)} custom-call(bf16[64,512]{1,0:T(8,128)(2,1)S(1)} %collective-permute-done.3.refs_0_, bf16[64,512]{1,0:T(8,128)(2,1)S(1)} %collective-permute-done.4.refs_1_, bf16[64,512]{1,0:T(8,128)(2,1)S(1)} %collective-permute-done.5.refs_2_, bf16[64,512]{1,0:T(8,128)(2,1)S(1)} %get-tuple-element.42.after_ref.refs_3_, ...), custom_call_target="tpu_custom_call" | custom-call | flops 500000000 | bytes 2000000 | tf_op jit(solution)/shard_map/near_score/pallas_call | solution.py:493
  20.8 0.6 %collective-permute-done.6.other_ref = bf16[128,512]{1,0:T(8,128)(2,1)S(1)} collective-permute-done((bf16[128,512]{1,0:T(8,128)(2,1)S(1)}, bf16[128,512]{1,0:T(8,128)(2,1)S(1)}, u32[]{:S(2)}, u32[]{:S(2)}) %collective-permute-start.6) | collective-permute-done | bytes 131104 | tf_op jit(solution)/shard_map/ppermute | solution.py:389
  21.4 0.4 %far_score.1.after_ref = f32[4,128]{1,0:T(4,128)S(1)} custom-call(f32[128,1]{1,0:T(8,128)S(1)} %near_score.1.near_ref, f32[128,512]{1,0:T(8,128)S(1)} %get-tuple-element.48.state_ref, bf16[128,512]{1,0:T(8,128)(2,1)S(1)} %get-tuple-element.49.mine_ref, bf16[128,512]{1,0:T(8,128)(2,1)S(1)} %collective-permute-done.6.other_ref, ...), custom_call_target="tpu_custom_call" | custom-call | flops 200000000 | bytes 1000000 | tf_op jit(solution)/shard_map/far_score/pallas_call | solution.py:502
  21.8 1.1 %collective-permute-start.8 = (f32[4,128]{1,0:T(4,128)S(1)}, f32[4,128]{1,0:T(4,128)S(1)}, u32[]{:S(2)}, u32[]{:S(2)}) collective-permute-start(f32[4,128]{1,0:T(4,128)S(1)} %far_score.1.after_ref), channel_id=1, source_target_pairs={{0,4},{2,6},{4,0},{6,2},{8,12},{10,14},{12,8},{14,10},{1,5},{3,7},... | collective-permute-start | bytes 6152 | tf_op jit(solution)/shard_map/ppermute | solution.py:451
  22.9 1.1 %ensemble.4.after_ref = f32[2,128]{1,0:T(2,128)S(1)} custom-call(bf16[1024,512]{1,0:T(8,128)(2,1)S(1)} %copy-done.1, bf16[2,512,1024]{2,1,0:T(8,128)(2,1)S(1)} %copy-done, f32[2,1024]{1,0:T(2,128)S(1)} %copy-done.3, bf16[2,1024]{1,0:T(2,128)(2,1)S(1)} %copy-done.4, f32[4,128]{1,0:T(4,128)S(1)} %far_score.1.after_ref), custom_call_target="tpu_custom_call" | custom-call | flops 536870912 | bytes 1000000 | tf_op jit(solution)/shard_map/ensemble/pallas_call | solution.py:467
  24.1 1.4 %collective-permute-done.8 = f32[4,128]{1,0:T(4,128)S(1)} collective-permute-done((f32[4,128]{1,0:T(4,128)S(1)}, f32[4,128]{1,0:T(4,128)S(1)}, u32[]{:S(2)}, u32[]{:S(2)}) %collective-permute-start.8) | collective-permute-done | bytes 2080 | tf_op jit(solution)/shard_map/ppermute | solution.py:451
  25.4 1.4 %collective-permute-start.9 = (f32[8,128]{1,0:T(8,128)S(1)}, f32[8,128]{1,0:T(8,128)S(1)}, u32[]{:S(2)}, u32[]{:S(2)}) collective-permute-start(f32[8,128]{1,0:T(8,128)S(1)} %pad_maximum_fusion), channel_id=1, source_target_pairs={{0,8},{2,10},{4,12},{6,14},{8,0},{10,2},{12,4},{14,6},{1,9},{3,11}... | collective-permute-start | bytes 12296 | tf_op jit(solution)/shard_map/ppermute | solution.py:451
  26.9 1.1 %ensemble.5 = f32[2,128]{1,0:T(2,128)S(1)} custom-call(bf16[1024,512]{1,0:T(8,128)(2,1)S(1)} %copy-done.1, bf16[2,512,1024]{2,1,0:T(8,128)(2,1)S(1)} %copy-done, f32[2,1024]{1,0:T(2,128)S(1)} %copy-done.3, bf16[2,1024]{1,0:T(2,128)(2,1)S(1)} %copy-done.4, f32[4,128]{1,0:T(4,128)S(1)} %far_score.1.after_ref), custom_call_target="tpu_custom_call" | custom-call | flops 536870912 | bytes 1000000 | tf_op jit(solution)/shard_map/ensemble/pallas_call | solution.py:467
  28.0 1.9 %collective-permute-done.9 = f32[8,128]{1,0:T(8,128)S(1)} collective-permute-done((f32[8,128]{1,0:T(8,128)S(1)}, f32[8,128]{1,0:T(8,128)S(1)}, u32[]{:S(2)}, u32[]{:S(2)}) %collective-permute-start.9) | collective-permute-done | bytes 4128 | tf_op jit(solution)/shard_map/ppermute | solution.py:451
  30.1 0.4 %expand.1 = (bf16[96,1024]{1,0:T(8,128)(2,1)S(1)}, s32[1,1024]{1,0:T(1,128)S(1)}) custom-call(s32[256,3]{1,0:T(8,128)S(1)} %get-tuple-element.30.where_ref, f32[2,128]{1,0:T(2,128)S(1)} %ensemble.4.after_ref), custom_call_target="tpu_custom_call" | custom-call | flops 100000000 | bytes 1000000 | tf_op jit(solution)/shard_map/expand/pallas_call | solution.py:524
  30.5 0.7 %collective-permute-done.10.far_ref = f32[24,128]{1,0:T(8,128)S(1)} collective-permute-done((f32[24,128]{1,0:T(8,128)S(1)}, f32[24,128]{1,0:T(8,128)S(1)}, u32[]{:S(2)}, u32[]{:S(2)}) %collective-permute-start.10) | collective-permute-done | bytes 12320 | tf_op jit(solution)/shard_map/ppermute | solution.py:389
  31.2 0.9 %finish.1 = f32[1,1024]{1,0:T(1,128)} custom-call(bf16[96,1024]{1,0:T(8,128)(2,1)S(1)} %get-tuple-element.50.line_ref, s32[1,1024]{1,0:T(1,128)S(1)} %get-tuple-element.51.lane_ref, f32[24,128]{1,0:T(8,128)S(1)} %concatenate.8.near_ref, f32[24,128]{1,0:T(8,128)S(1)} %collective-permute-done.10.far_ref), custom_call_target="tpu_custom_call" | custom-call | flops 1000000 | bytes 1000000 | tf_op jit(solution)/shard_map/finish/pallas_call | solution.py:534
  (38 shorter events, 0.5 us)
Async XLA Ops:
  0.0 2.6 %copy-start = (bf16[2,512,1024]{2,1,0:T(8,128)(2,1)S(1)}, bf16[2,512,1024]{2,1,0:T(8,128)(2,1)}, u32[]{:S(2)}) copy-start(bf16[2,512,1024]{2,1,0:T(8,128)(2,1)} %w_ref.7) | copy-start | bytes 6291460
  0.0 2.6 %copy-start.3 = (f32[2,1024]{1,0:T(2,128)S(1)}, f32[2,1024]{1,0:T(2,128)}, u32[]{:S(2)}) copy-start(f32[2,1024]{1,0:T(2,128)} %bias_ref.7) | copy-start | bytes 24580
  0.0 2.6 %copy-start.4 = (bf16[2,1024]{1,0:T(2,128)(2,1)S(1)}, bf16[2,1024]{1,0:T(2,128)(2,1)}, u32[]{:S(2)}) copy-start(bf16[2,1024]{1,0:T(2,128)(2,1)} %out_ref.7) | copy-start | bytes 12292
  0.0 2.6 %copy-start.11 = (f32[1,512]{1,0:T(1,128)S(1)}, f32[1,512]{1,0:T(1,128)}, u32[]{:S(2)}) copy-start(f32[1,512]{1,0:T(1,128)} %upb_ref.1) | copy-start | bytes 6148
  0.0 2.6 %copy-start.12 = (f32[1,512]{1,0:T(1,128)S(1)}, f32[1,512]{1,0:T(1,128)}, u32[]{:S(2)}) copy-start(f32[1,512]{1,0:T(1,128)} %head_ref.1) | copy-start | bytes 6148
  0.0 7.2 %collective-permute-start = (bf16[3,512,256]{2,1,0:T(8,128)(2,1)}, bf16[3,512,256]{2,1,0:T(8,128)(2,1)S(1)}, u32[]{:S(2)}, u32[]{:S(2)}) collective-permute-start(bf16[3,512,256]{2,1,0:T(8,128)(2,1)} %q0_ref.3), channel_id=1, source_target_pairs={{0,1},{1,0},{2,3},{3,2},{4,5},{5,4},{6,7},{7,6},{8,9},{9,8},{10,11... | collective-permute-start | bytes 2359304 | tf_op jit(solution)/shard_map/ppermute | solution.py:389
  2.5 4.8 %copy-start.2 = (bf16[3,512,256]{2,1,0:T(8,128)(2,1)S(1)}, bf16[3,512,256]{2,1,0:T(8,128)(2,1)}, u32[]{:S(2)}) copy-start(bf16[3,512,256]{2,1,0:T(8,128)(2,1)} %q0_ref.3) | copy-start | bytes 2359300
  2.5 4.7 %copy-start.5 = (f32[4,512]{1,0:T(4,128)S(1)}, f32[4,512]{1,0:T(4,128)}, u32[]{:S(2)}) copy-start(f32[4,512]{1,0:T(4,128)} %scale_ref.1) | copy-start | bytes 24580
  2.5 4.7 %copy-start.6 = (f32[4,512]{1,0:T(4,128)S(1)}, f32[4,512]{1,0:T(4,128)}, u32[]{:S(2)}) copy-start(f32[4,512]{1,0:T(4,128)} %shift_ref.1) | copy-start | bytes 24580
  2.5 4.7 %copy-start.7 = (f32[512]{0:T(512)S(1)}, f32[512]{0:T(512)}, u32[]{:S(2)}) copy-start(f32[512]{0:T(512)} %param.29) | copy-start | bytes 6148
  2.5 4.7 %copy-start.8 = (f32[512]{0:T(512)S(1)}, f32[512]{0:T(512)}, u32[]{:S(2)}) copy-start(f32[512]{0:T(512)} %param.30) | copy-start | bytes 6148
  2.5 4.7 %copy-start.9 = (f32[512]{0:T(512)S(1)}, f32[512]{0:T(512)}, u32[]{:S(2)}) copy-start(f32[512]{0:T(512)} %param.26) | copy-start | bytes 6148
  2.5 4.7 %copy-start.10 = (f32[512]{0:T(512)S(1)}, f32[512]{0:T(512)}, u32[]{:S(2)}) copy-start(f32[512]{0:T(512)} %param.33) | copy-start | bytes 6148
  3.9 4.1 %collective-permute-start.1 = (bf16[528,512]{1,0:T(8,128)(2,1)S(1)}, bf16[528,512]{1,0:T(8,128)(2,1)S(1)}, u32[]{:S(2)}, u32[]{:S(2)}) collective-permute-start(bf16[528,512]{1,0:T(8,128)(2,1)S(1)} %get-tuple-element.35.refs_3_), channel_id=1, source_target_pairs={{0,1},{1,0},{2,3},{3,2},{4,5},{5,4},{6,7},{7,6},{8,9},{9,8},{10,11... | collective-permute-start | bytes 1622024 | tf_op jit(solution)/shard_map/ppermute | solution.py:389
  4.2 3.8 %collective-permute-start.2 = (bf16[512,512]{1,0:T(8,128)(2,1)S(1)}, bf16[512,512]{1,0:T(8,128)(2,1)S(1)}, u32[]{:S(2)}, u32[]{:S(2)}) collective-permute-start(bf16[512,512]{1,0:T(8,128)(2,1)S(1)} %get-tuple-element.38.fw0_ref.refs_1_), channel_id=1, source_target_pairs={{0,1},{1,0},{2,3},{3,2},{4,5},{5,4},{6,7},{7,6},{8,9},{9,8},{10,11... | collective-permute-start | bytes 1572872 | tf_op jit(solution)/shard_map/ppermute | solution.py:389
  4.5 16.3 %collective-permute-start.7 = (bf16[528,512]{1,0:T(8,128)(2,1)S(1)}, bf16[528,512]{1,0:T(8,128)(2,1)S(1)}, u32[]{:S(2)}, u32[]{:S(2)}) collective-permute-start(bf16[528,512]{1,0:T(8,128)(2,1)S(1)} %get-tuple-element.35.refs_3_), channel_id=1, source_target_pairs={{0,2},{2,0},{4,6},{6,4},{8,10},{10,8},{12,14},{14,12},{1,3},{3,1},... | collective-permute-start | bytes 1622024 | tf_op jit(solution)/shard_map/ppermute | solution.py:425
  8.0 6.5 %copy-start.1 = (bf16[1024,512]{1,0:T(8,128)(2,1)S(1)}, bf16[1024,512]{1,0:T(8,128)(2,1)}, u32[]{:S(2)}) copy-start(bf16[1024,512]{1,0:T(8,128)(2,1)} %feat_ref.5) | copy-start | bytes 3145732
  10.1 6.8 %collective-permute-start.3 = (bf16[64,512]{1,0:T(8,128)(2,1)S(1)}, bf16[64,512]{1,0:T(8,128)(2,1)S(1)}, u32[]{:S(2)}, u32[]{:S(2)}) collective-permute-start(bf16[64,512]{1,0:T(8,128)(2,1)S(1)} %get-tuple-element.39), channel_id=1, source_target_pairs={{0,12},{2,14},{4,8},{6,10},{8,4},{10,6},{12,0},{14,2},{1,13},{3,15... | collective-permute-start | bytes 196616 | tf_op jit(solution)/shard_map/ppermute | solution.py:451
  13.8 5.7 %collective-permute-start.4 = (bf16[64,512]{1,0:T(8,128)(2,1)S(1)}, bf16[64,512]{1,0:T(8,128)(2,1)S(1)}, u32[]{:S(2)}, u32[]{:S(2)}) collective-permute-start(bf16[64,512]{1,0:T(8,128)(2,1)S(1)} %get-tuple-element.40), channel_id=1, source_target_pairs={{0,8},{2,10},{4,12},{6,14},{8,0},{10,2},{12,4},{14,6},{1,9},{3,11}... | collective-permute-start | bytes 196616 | tf_op jit(solution)/shard_map/ppermute | solution.py:451
  13.8 5.7 %collective-permute-start.5 = (bf16[64,512]{1,0:T(8,128)(2,1)S(1)}, bf16[64,512]{1,0:T(8,128)(2,1)S(1)}, u32[]{:S(2)}, u32[]{:S(2)}) collective-permute-start(bf16[64,512]{1,0:T(8,128)(2,1)S(1)} %get-tuple-element.41), channel_id=1, source_target_pairs={{0,4},{2,6},{4,0},{6,2},{8,12},{10,14},{12,8},{14,10},{1,5},{3,7},... | collective-permute-start | bytes 196616 | tf_op jit(solution)/shard_map/ppermute | solution.py:451
  19.9 1.4 %collective-permute-start.6 = (bf16[128,512]{1,0:T(8,128)(2,1)S(1)}, bf16[128,512]{1,0:T(8,128)(2,1)S(1)}, u32[]{:S(2)}, u32[]{:S(2)}) collective-permute-start(bf16[128,512]{1,0:T(8,128)(2,1)S(1)} %get-tuple-element.49.mine_ref), channel_id=1, source_target_pairs={{0,1},{1,0},{2,3},{3,2},{4,5},{5,4},{6,7},{7,6},{8,9},{9,8},{10,11... | collective-permute-start | bytes 393224 | tf_op jit(solution)/shard_map/ppermute | solution.py:389
  21.8 3.7 %collective-permute-start.8 = (f32[4,128]{1,0:T(4,128)S(1)}, f32[4,128]{1,0:T(4,128)S(1)}, u32[]{:S(2)}, u32[]{:S(2)}) collective-permute-start(f32[4,128]{1,0:T(4,128)S(1)} %far_score.1.after_ref), channel_id=1, source_target_pairs={{0,4},{2,6},{4,0},{6,2},{8,12},{10,14},{12,8},{14,10},{1,5},{3,7},... | collective-permute-start | bytes 6152 | tf_op jit(solution)/shard_map/ppermute | solution.py:451
  25.4 4.5 %collective-permute-start.9 = (f32[8,128]{1,0:T(8,128)S(1)}, f32[8,128]{1,0:T(8,128)S(1)}, u32[]{:S(2)}, u32[]{:S(2)}) collective-permute-start(f32[8,128]{1,0:T(8,128)S(1)} %pad_maximum_fusion), channel_id=1, source_target_pairs={{0,8},{2,10},{4,12},{6,14},{8,0},{10,2},{12,4},{14,6},{1,9},{3,11}... | collective-permute-start | bytes 12296 | tf_op jit(solution)/shard_map/ppermute | solution.py:451
  30.0 1.2 %collective-permute-start.10 = (f32[24,128]{1,0:T(8,128)S(1)}, f32[24,128]{1,0:T(8,128)S(1)}, u32[]{:S(2)}, u32[]{:S(2)}) collective-permute-start(f32[24,128]{1,0:T(8,128)S(1)} %concatenate.8.near_ref), channel_id=1, source_target_pairs={{0,1},{1,0},{2,3},{3,2},{4,5},{5,4},{6,7},{7,6},{8,9},{9,8},{10,11... | collective-permute-start | bytes 36872 | tf_op jit(solution)/shard_map/ppermute | solution.py:389

commit v3 on v1

--- a/solution.py
+++ b/solution.py
@@ -74,13 +74,16 @@
 
 def route_kernel(
     n, half, relative, esc_hbm, own_hbm, feat_hbm, down_hbm, up_hbm, fw_hbm, ow_hbm,
-    index_ref, rows_ref, down_ref, segment_ref, both_ref, esc_ref, own_ref, feat_ref, sems,
+    index_ref, rows_ref, down_ref, segment_ref, bundle_ref, esc_ref, own_ref, feat_ref, sems,
 ):
+    depth = up_hbm.shape[1]
     copies = start_all(
         [(esc_hbm, esc_ref), (own_hbm, own_ref), (feat_hbm, feat_ref), (down_hbm.at[0], down_ref),
-         (fw_hbm, both_ref.at[: fw_hbm.shape[0]]), (ow_hbm, both_ref.at[fw_hbm.shape[0] :]),
-         (up_hbm.at[0], segment_ref.at[: up_hbm.shape[1]])], sems)
-    segment_ref[up_hbm.shape[1] :, :] = jnp.zeros((EXTRA, up_hbm.shape[2]), BF)
+         (up_hbm.at[0], segment_ref.at[:depth]), (up_hbm.at[0], bundle_ref.at[:depth]),
+         (fw_hbm, bundle_ref.at[pl.ds(depth + EXTRA, fw_hbm.shape[0])]),
+         (ow_hbm, bundle_ref.at[pl.ds(depth + EXTRA + fw_hbm.shape[0], ow_hbm.shape[0])])], sems)
+    for ref in (segment_ref, bundle_ref):
+        ref[depth : depth + EXTRA, :] = jnp.zeros((EXTRA, up_hbm.shape[2]), BF)
     core = lax.axis_index("member")
     count = esc_hbm.shape[1]
     dealt = count // 2
@@ -113,8 +116,8 @@
 
 
 def predict_kernel(
-    rows_ref, w_ref, bias_ref, out_ref, upb_ref, head_ref, down_ref, raw_ref,
-    near_ref, segment_ref,
+    rows_ref, w_ref, bias_ref, out_ref, upb_ref, head_ref, down_ref, raw_ref, raw_bundle_ref, after_ref,
+    near_ref, segment_ref, bundle_ref,
 ):
     depth = raw_ref.shape[0] - EXTRA
     here = w_ref.shape[0]
@@ -136,7 +139,8 @@
     members = EXTRA - PREDS
     far = jnp.concatenate([preds[:members, dealt:], jnp.zeros((members, down.shape[1] - dealt), F32)], axis=1)
     extra.append(far)
-    segment_ref[depth:, :] = jnp.concatenate(extra, axis=0).astype(BF)
+    for ref in (segment_ref, bundle_ref):
+        ref[depth : depth + EXTRA, :] = jnp.concatenate(extra, axis=0).astype(BF)
 
 
 def constants_kernel(
@@ -182,6 +186,11 @@
     table_ref[LCLS : LCLS + 1, :LANES] = jnp.sum(jnp.where(eye, logits, 0.0), axis=0, keepdims=True)
 
 
+def feature_half(bundle_ref, rows):
+    first = bundle_ref.shape[1] + EXTRA
+    return bundle_ref[first : first + rows]
+
+
 def attend_kernel(
     members, rows_ref, near_ref, other_ref, place_ref, table_ref, fw0_ref, fw1_ref, q0_ref, q1_ref, *sent_refs
 ):
@@ -194,10 +203,10 @@
     low, high = rows[:, : fwidth // 2].astype(F32), rows[:, fwidth // 2 :].astype(F32)
     first = jnp.where(core == 0, low, high).astype(BF)
     second = jnp.where(core == 0, high, low).astype(BF)
-    token = dot(first, fw0_ref[: fwidth // 2]) + dot(second, fw1_ref[: fwidth // 2]) + table_ref[FBIAS : FBIAS + 1, :]
+    token = dot(first, feature_half(fw0_ref, fwidth // 2)) + dot(second, feature_half(fw1_ref, fwidth // 2)) + table_ref[FBIAS : FBIAS + 1, :]
     centered = centre(token)
     tokens = [(centered * inverse_spread(centered) * gain).astype(BF)]
-    first = other_ref.shape[0] - EXTRA + PREDS
+    first = table_ref.shape[1] + PREDS
     far = other_ref[first : first + EXTRA - PREDS, :total].astype(F32)
     preds = (near_ref[...] + jnp.concatenate([far, jnp.zeros((8 - far.shape[0], total), F32)], axis=0)).T
     for m in range(members):
@@ -255,9 +264,8 @@
         copy.wait()
 
 
-def unpack(ref):
-    depth = ref.shape[0] - EXTRA
-    extra = ref[depth:, :].astype(F32)
+def unpack(ref, depth):
+    extra = ref[depth : depth + EXTRA, :].astype(F32)
     return ref[:depth, :], *(jnp.sum(extra[i : i + 3], axis=0, keepdims=True) for i in (DOWN, BIAS, HEAD))
 
 
@@ -286,18 +294,18 @@
 
 
 def near_score_kernel(blocks, half, *refs):
-    table_ref, both0_ref, both1_ref, up0_ref, up1_ref, score_ref = refs[blocks:]
+    table_ref, both0_ref, both1_ref, score_ref = refs[blocks:]
     state, normed = states(arrived(refs[:blocks][::-1], half, 0), table_ref, both0_ref, both1_ref)
-    up, down, bias, head = unpack(up0_ref)
+    up, down, bias, head = unpack(both0_ref, normed.shape[1])
     terms = state * head + hidden_terms(normed, up, down, bias)
-    up, down, bias, _ = unpack(up1_ref)
+    up, down, bias, _ = unpack(both1_ref, normed.shape[1])
     terms = terms + hidden_terms(normed, up, down, bias)
     score_ref[...] = jnp.sum(terms, axis=-1, keepdims=True)
 
 
 def far_score_kernel(blocks, half, near_ref, state_ref, mine_ref, other_ref, up2_ref, out_ref):
     rows = near_ref.shape[0]
-    up, down, bias, head = unpack(up2_ref)
+    up, down, bias, head = unpack(up2_ref, mine_ref.shape[1])
     terms = hidden_terms(jnp.concatenate([mine_ref[...], other_ref[...]], axis=0), up, down, bias)
     scores = [
         near_ref[...],
@@ -390,31 +398,30 @@
 
     dealt = count // 2
     ins = (escalated, owners, features, down_weight, up_weight, feat_weight, out_weight)
-    index, mine, down, segment, own_both = pl.pallas_call(
+    index, mine, down, segment, bundle = pl.pallas_call(
         functools.partial(route_kernel, n, half, relative),
         out_shape=[shape((8, count), jnp.int32), shape((count, fwidth), BF), shape(down_weight.shape[1:], BF),
                    shape((up_weight.shape[1] + EXTRA, up_weight.shape[2]), BF),
-                   shape((feat_weight.shape[0] + out_weight.shape[0], width), BF)],
+                   shape((up_weight.shape[1] + EXTRA + feat_weight.shape[0] + out_weight.shape[0], width), BF)],
         in_specs=[HBM] * len(ins),
         out_specs=[VMEM] * 5,
-        scratch_shapes=[pltpu.VMEM(x.shape, x.dtype) for x in ins[:3]] + [pltpu.SemaphoreType.DMA((7,))],
+        scratch_shapes=[pltpu.VMEM(x.shape, x.dtype) for x in ins[:3]] + [pltpu.SemaphoreType.DMA((8,))],
         compiler_params=params(24),
         cost_estimate=cost(2 * count * rows * fwidth, 3 * 10**6),
         name="route",
     )(*in_hbm(ins))
-    near, segment = pl.pallas_call(
+    near, segment, bundle = pl.pallas_call(
         predict_kernel,
-        out_shape=[shape((8, dealt), F32), shape(segment.shape, BF)],
-        in_specs=[VMEM] * 8,
-        out_specs=[VMEM] * 2,
-        input_output_aliases={7: 1},
+        out_shape=[shape((8, dealt), F32), shape(segment.shape, BF), shape(bundle.shape, BF)],
+        in_specs=[VMEM] * 9 + [ANY],
+        out_specs=[VMEM] * 3,
+        input_output_aliases={7: 1, 8: 2},
         compiler_params=params(24),
         cost_estimate=cost(2 * here * count * fwidth * hidden, 3 * 10**6, here * count * hidden),
         name="predict",
-    )(mine, member_in, member_bias, member_out, up_bias, owner_heads, down, segment)
-    other_both = swap(own_both)
+    )(mine, member_in, member_bias, member_out, up_bias, owner_heads, down, segment, bundle, other_qkv)
+    other_bundle = swap(bundle)
     next_segment = lax.ppermute(segment, "rows", [(i, i ^ 1) for i in range(n)])
-    other_segment = swap(segment)
 
     ins = (cls_token, attn_gain, pred_scale, pred_shift, feat_bias, ffn_gain, qkv_weight, other_qkv, index)
     table, where, place = pl.pallas_call(
@@ -436,7 +443,7 @@
         compiler_params=params(24),
         cost_estimate=cost(10**9, 2 * 10**6),
         name="attend",
-    )(mine, near, other_segment, place, table, own_both, other_both, qkv_weight, other_qkv)
+    )(mine, near, other_bundle, place, table, bundle, other_bundle, qkv_weight, other_qkv)
 
     def across(x, k):
         return lax.ppermute(x, "rows", [(i, i ^ (2 * k)) for i in range(n)])
@@ -467,8 +474,7 @@
         )(features, member_in, member_bias, member_out, after, *held)
 
     early = (tiles + 1) // 2
-    preds, table, both0, both1, up0, up1 = ensemble(
-        0, early, sent[0], (table, own_both, other_both, segment, other_segment))
+    preds, table, bundle, other_bundle = ensemble(0, early, sent[0], (table, bundle, other_bundle))
     preds = [preds]
 
     state, next_rows = pl.pallas_call(
@@ -479,17 +485,17 @@
         compiler_params=params(24),
         cost_estimate=cost(2 * 10**8, 2 * 10**6),
         name="arrive",
-    )(*got[::-1], table, both0, both1)
+    )(*got[::-1], table, bundle, other_bundle)
     other_rows = swap(next_rows)
     near_scores = pl.pallas_call(
         functools.partial(near_score_kernel, blocks, half),
         out_shape=shape((slots // 2, 1), F32),
-        in_specs=[VMEM] * (blocks + 5),
+        in_specs=[VMEM] * (blocks + 3),
         out_specs=VMEM,
         compiler_params=params(24),
         cost_estimate=cost(5 * 10**8, 2 * 10**6),
         name="near_score",
-    )(*got[::-1], table, both0, both1, up0, up1)
+    )(*got[::-1], table, bundle, other_bundle)
     scores = pl.pallas_call(
         functools.partial(far_score_kernel, blocks, half),
         out_shape=shape((blocks, LANES if relative else 3 * slots // 2), F32),

time: 32.4 us -> 32.8 us (1.012)
  local copies, waits for them, and re-layouts: 0.11 us -> 0.55 us
  starting transfers between devices: 11 us -> 10.6 us
    ppermute x5 -> x4, starting transfers between devices: 1.18 us -> 0.65 us  [swap(): return lax.ppermute(x, 'member', [(0, 1), (1, 0)])]
    unnamed x26, local copies, waits for them, and re-layouts: 0.07 us -> 0.51 us
    ppermute x5 -> x4, waiting for transfers between devices: 1.29 us -> 1.31 us  [swap(): return lax.ppermute(x, 'member', [(0, 1), (1, 0)])]
  transfers between devices with their start and end apart: 11 -> 10, of which waited for: 5 -> 5; matrix products, arithmetic and copies ran while one was open for 0% -> 0% of each run, Pallas kernels for 38% -> 34%
where the time goes in v3:
time: 32.8 us; the launch traced here: 32.7 us
  Pallas kernels  13.9 us (42%)
  starting transfers between devices  10.6 us (32%)
  waiting for transfers between devices  7.45 us (23%)
  local copies, waits for them, and re-layouts  0.55 us (2%)
    ppermute x5, starting transfers between devices, across(): return lax.ppermute(x, 'rows', [(i, i ^ 2 * k) for i in range(n)])  7.03 us
    ppermute x5, waiting for transfers between devices, across(): return lax.ppermute(x, 'rows', [(i, i ^ 2 * k) for i in range(n)])  6.13 us
    pallas_call x3, Pallas kernels, ensemble(): pl.pallas_call(functools.partial(ensemble_kernel, first, number, tile), o...  4.64 us
    ppermute x1, starting transfers between devices, per_device(): next_segment = lax.ppermute(segment, 'rows', [(i, i ^ 1) for i in range(n)])  2.94 us
    pallas_call x1, Pallas kernels, per_device(): pl.pallas_call(functools.partial(attend_kernel, members), out_shape=[shap...  2.11 us
    pallas_call x1, Pallas kernels, per_device(): pl.pallas_call(functools.partial(route_kernel, n, half, relative), out_sh...  2.07 us
    pallas_call x1, Pallas kernels, per_device(): pl.pallas_call(predict_kernel, out_shape=[shape((8, dealt), F32), shape(s...  1.35 us
    ppermute x4, waiting for transfers between devices, swap(): return lax.ppermute(x, 'member', [(0, 1), (1, 0)])  1.31 us
  transfers between devices with their start and end apart: 10, of which 5 were waited for; matrix products, arithmetic and copies ran while one was open for 0% of the time, Pallas kernels for 34%

profile of v3, /device:TPU:0, one launch (start us, length us, event | category | flops | bytes accessed | tf_op | source)
XLA Modules:
  0.0 32.7 jit_solution(8500205521813347892)
XLA Ops:
  0.0 0.5 %collective-permute-start = (bf16[3,512,256]{2,1,0:T(8,128)(2,1)}, bf16[3,512,256]{2,1,0:T(8,128)(2,1)S(1)}, u32[]{:S(2)}, u32[]{:S(2)}) collective-permute-start(bf16[3,512,256]{2,1,0:T(8,128)(2,1)} %q0_ref.3), channel_id=1, source_target_pairs={{0,1},{1,0},{2,3},{3,2},{4,5},{5,4},{6,7},{7,6},{8,9},{9,8},{10,11... | collective-permute-start | bytes 2359304 | tf_op jit(solution)/shard_map/ppermute | solution.py:388
  0.5 2.1 %route.1 = (s32[8,256]{1,0:T(8,128)S(1)}, bf16[256,512]{1,0:T(8,128)(2,1)S(1)}, bf16[512,512]{1,0:T(8,128)(2,1)S(1)}, bf16[528,512]{1,0:T(8,128)(2,1)S(1)}, bf16[1040,512]{1,0:T(8,128)(2,1)S(1)}) custom-call(s32[1,256]{1,0:T(1,128)} %esc_hbm.1, s32[1,256]{1,0:T(1,128)} %bitcast.10, bf16[1024,512]{1,0:T(8,128)(2,1)} %feat_ref.5, ...), custom_call_target="tpu_custom_call" | custom-call | flops 268435456 | bytes 3000000 | tf_op jit(solution)/shard_map/route/pallas_call | solution.py:401
  2.6 0.4 %copy-done = bf16[2,512,1024]{2,1,0:T(8,128)(2,1)S(1)} copy-done((bf16[2,512,1024]{2,1,0:T(8,128)(2,1)S(1)}, bf16[2,512,1024]{2,1,0:T(8,128)(2,1)}, u32[]{:S(2)}) %copy-start) | copy-done | bytes 2097176
  3.1 1.3 %predict.1 = (f32[8,128]{1,0:T(8,128)S(1)}, bf16[528,512]{1,0:T(8,128)(2,1)S(1)}, bf16[1040,512]{1,0:T(8,128)(2,1)S(1)}) custom-call(bf16[256,512]{1,0:T(8,128)(2,1)S(1)} %get-tuple-element.30.rows_ref, bf16[2,512,1024]{2,1,0:T(8,128)(2,1)S(1)} %copy-done, f32[2,1024]{1,0:T(2,128)S(1)} %copy-done.3, ...), custom_call_target="tpu_custom_call", output_to_operand_aliasing={{1}: (7, {}), {2}: (8, {})} | custom-call | flops 536870912 | bytes 3000000 | tf_op jit(solution)/shard_map/predict/pallas_call | solution.py:413
  4.5 2.9 %collective-permute-start.6 = (bf16[528,512]{1,0:T(8,128)(2,1)S(1)}, bf16[528,512]{1,0:T(8,128)(2,1)S(1)}, u32[]{:S(2)}, u32[]{:S(2)}) collective-permute-start(bf16[528,512]{1,0:T(8,128)(2,1)S(1)} %get-tuple-element.47), channel_id=1, source_target_pairs={{0,2},{2,0},{4,6},{6,4},{8,10},{10,8},{12,14},{14,12},{1,3},{3,1},... | collective-permute-start | bytes 1622024 | tf_op jit(solution)/shard_map/ppermute | solution.py:424
  7.5 0.7 %constants.1 = (f32[40,512]{1,0:T(8,128)S(1)}, s32[256,3]{1,0:T(8,128)S(1)}, s32[1,128]{1,0:T(1,128)S(1)}) custom-call(f32[1,512]{1,0:T(1,128)S(1)} %bitcast.6, f32[1,512]{1,0:T(1,128)S(1)} %bitcast.7, f32[4,512]{1,0:T(4,128)S(1)} %copy-done.5, f32[4,512]{1,0:T(4,128)S(1)} %copy-done.6, f32[1,512]{1,0:T(1,128)S(1)} %bitcast.8, f32[1,512]{1,0:T(1,128)S(1)} %bitcast.9, ...), custom_call_target="tpu_custom_call" | custom-call | flops 100000000 | bytes 2000000 | tf_op jit(solution)/shard_map/constants/pallas_call | solution.py:427
  8.3 2.1 %attend.1 = (bf16[64,512]{1,0:T(8,128)(2,1)S(1)}, bf16[64,512]{1,0:T(8,128)(2,1)S(1)}, bf16[64,512]{1,0:T(8,128)(2,1)S(1)}, bf16[64,512]{1,0:T(8,128)(2,1)S(1)}) custom-call(bf16[256,512]{1,0:T(8,128)(2,1)S(1)} %get-tuple-element.30.rows_ref, f32[8,128]{1,0:T(8,128)S(1)} %get-tuple-element.34.near_ref, ...), custom_call_target="tpu_custom_call" | custom-call | flops 1000000000 | bytes 2000000 | tf_op jit(solution)/shard_map/attend/pallas_call | solution.py:438
  10.4 3.7 %collective-permute-start.2 = (bf16[64,512]{1,0:T(8,128)(2,1)S(1)}, bf16[64,512]{1,0:T(8,128)(2,1)S(1)}, u32[]{:S(2)}, u32[]{:S(2)}) collective-permute-start(bf16[64,512]{1,0:T(8,128)(2,1)S(1)} %get-tuple-element.38), channel_id=1, source_target_pairs={{0,12},{2,14},{4,8},{6,10},{8,4},{10,6},{12,0},{14,2},{1,13},{3,15... | collective-permute-start | bytes 196616 | tf_op jit(solution)/shard_map/ppermute | solution.py:449
  14.1 0.8 %collective-permute-start.4 = (bf16[64,512]{1,0:T(8,128)(2,1)S(1)}, bf16[64,512]{1,0:T(8,128)(2,1)S(1)}, u32[]{:S(2)}, u32[]{:S(2)}) collective-permute-start(bf16[64,512]{1,0:T(8,128)(2,1)S(1)} %get-tuple-element.40), channel_id=1, source_target_pairs={{0,4},{2,6},{4,0},{6,2},{8,12},{10,14},{12,8},{14,10},{1,5},{3,7},... | collective-permute-start | bytes 196616 | tf_op jit(solution)/shard_map/ppermute | solution.py:449
  14.9 2.4 %ensemble.3 = (f32[4,128]{1,0:T(4,128)S(1)}, f32[40,512]{1,0:T(8,128)S(1)}, bf16[1040,512]{1,0:T(8,128)(2,1)S(1)}, bf16[1040,512]{1,0:T(8,128)(2,1)S(1)}) custom-call(bf16[1024,512]{1,0:T(8,128)(2,1)S(1)} %copy-done.1, bf16[2,512,1024]{2,1,0:T(8,128)(2,1)S(1)} %copy-done, f32[2,1024]{1,0:T(2,128)S(1)} %copy-done.3, bf16[2,1024]{1,0:T(2,128)(2,1)S(1)} %copy-done.4, ...), custom_call_target="tpu_custom_call" | custom-call | flops 1073741824 | bytes 1000000 | tf_op jit(solution)/shard_map/ensemble/pallas_call | solution.py:465
  17.2 2.8 %collective-permute-done.3.refs_1_ = bf16[64,512]{1,0:T(8,128)(2,1)S(1)} collective-permute-done((bf16[64,512]{1,0:T(8,128)(2,1)S(1)}, bf16[64,512]{1,0:T(8,128)(2,1)S(1)}, u32[]{:S(2)}, u32[]{:S(2)}) %collective-permute-start.3) | collective-permute-done | bytes 65568 | tf_op jit(solution)/shard_map/ppermute | solution.py:449
  20.1 0.4 %arrive.1 = (f32[128,512]{1,0:T(8,128)S(1)}, bf16[128,512]{1,0:T(8,128)(2,1)S(1)}) custom-call(bf16[64,512]{1,0:T(8,128)(2,1)S(1)} %collective-permute-done.2.refs_0_, bf16[64,512]{1,0:T(8,128)(2,1)S(1)} %collective-permute-done.3.refs_1_, bf16[64,512]{1,0:T(8,128)(2,1)S(1)} %collective-permute-done.4.refs_2_, ...), custom_call_target="tpu_custom_call" | custom-call | flops 200000000 | bytes 2000000 | tf_op jit(solution)/shard_map/arrive/pallas_call | solution.py:480
  20.6 0.8 %near_score.1.near_ref = f32[128,1]{1,0:T(8,128)S(1)} custom-call(bf16[64,512]{1,0:T(8,128)(2,1)S(1)} %collective-permute-done.2.refs_0_, bf16[64,512]{1,0:T(8,128)(2,1)S(1)} %collective-permute-done.3.refs_1_, bf16[64,512]{1,0:T(8,128)(2,1)S(1)} %collective-permute-done.4.refs_2_, bf16[64,512]{1,0:T(8,128)(2,1)S(1)} %get-tuple-element.41.after_ref.refs_3_, ...), custom_call_target="tpu_custom_call" | custom-call | flops 500000000 | bytes 2000000 | tf_op jit(solution)/shard_map/near_score/pallas_call | solution.py:490
  21.3 0.6 %collective-permute-done.5.other_ref = bf16[128,512]{1,0:T(8,128)(2,1)S(1)} collective-permute-done((bf16[128,512]{1,0:T(8,128)(2,1)S(1)}, bf16[128,512]{1,0:T(8,128)(2,1)S(1)}, u32[]{:S(2)}, u32[]{:S(2)}) %collective-permute-start.5) | collective-permute-done | bytes 131104 | tf_op jit(solution)/shard_map/ppermute | solution.py:388
  21.9 0.4 %far_score.1.after_ref = f32[4,128]{1,0:T(4,128)S(1)} custom-call(f32[128,1]{1,0:T(8,128)S(1)} %near_score.1.near_ref, f32[128,512]{1,0:T(8,128)S(1)} %get-tuple-element.45.state_ref, bf16[128,512]{1,0:T(8,128)(2,1)S(1)} %get-tuple-element.46.mine_ref, bf16[128,512]{1,0:T(8,128)(2,1)S(1)} %collective-permute-done.5.other_ref, ...), custom_call_target="tpu_custom_call" | custom-call | flops 200000000 | bytes 1000000 | tf_op jit(solution)/shard_map/far_score/pallas_call | solution.py:499
  22.3 1.3 %collective-permute-start.7 = (f32[4,128]{1,0:T(4,128)S(1)}, f32[4,128]{1,0:T(4,128)S(1)}, u32[]{:S(2)}, u32[]{:S(2)}) collective-permute-start(f32[4,128]{1,0:T(4,128)S(1)} %far_score.1.after_ref), channel_id=1, source_target_pairs={{0,4},{2,6},{4,0},{6,2},{8,12},{10,14},{12,8},{14,10},{1,5},{3,7},... | collective-permute-start | bytes 6152 | tf_op jit(solution)/shard_map/ppermute | solution.py:449
  23.6 1.1 %ensemble.4.after_ref = f32[2,128]{1,0:T(2,128)S(1)} custom-call(bf16[1024,512]{1,0:T(8,128)(2,1)S(1)} %copy-done.1, bf16[2,512,1024]{2,1,0:T(8,128)(2,1)S(1)} %copy-done, f32[2,1024]{1,0:T(2,128)S(1)} %copy-done.3, bf16[2,1024]{1,0:T(2,128)(2,1)S(1)} %copy-done.4, f32[4,128]{1,0:T(4,128)S(1)} %far_score.1.after_ref), custom_call_target="tpu_custom_call" | custom-call | flops 536870912 | bytes 1000000 | tf_op jit(solution)/shard_map/ensemble/pallas_call | solution.py:465
  24.8 1.2 %collective-permute-done.7 = f32[4,128]{1,0:T(4,128)S(1)} collective-permute-done((f32[4,128]{1,0:T(4,128)S(1)}, f32[4,128]{1,0:T(4,128)S(1)}, u32[]{:S(2)}, u32[]{:S(2)}) %collective-permute-start.7) | collective-permute-done | bytes 2080 | tf_op jit(solution)/shard_map/ppermute | solution.py:449
  26.0 1.3 %collective-permute-start.8 = (f32[8,128]{1,0:T(8,128)S(1)}, f32[8,128]{1,0:T(8,128)S(1)}, u32[]{:S(2)}, u32[]{:S(2)}) collective-permute-start(f32[8,128]{1,0:T(8,128)S(1)} %pad_maximum_fusion), channel_id=1, source_target_pairs={{0,8},{2,10},{4,12},{6,14},{8,0},{10,2},{12,4},{14,6},{1,9},{3,11}... | collective-permute-start | bytes 12296 | tf_op jit(solution)/shard_map/ppermute | solution.py:449
  27.3 1.1 %ensemble.5 = f32[2,128]{1,0:T(2,128)S(1)} custom-call(bf16[1024,512]{1,0:T(8,128)(2,1)S(1)} %copy-done.1, bf16[2,512,1024]{2,1,0:T(8,128)(2,1)S(1)} %copy-done, f32[2,1024]{1,0:T(2,128)S(1)} %copy-done.3, bf16[2,1024]{1,0:T(2,128)(2,1)S(1)} %copy-done.4, f32[4,128]{1,0:T(4,128)S(1)} %far_score.1.after_ref), custom_call_target="tpu_custom_call" | custom-call | flops 536870912 | bytes 1000000 | tf_op jit(solution)/shard_map/ensemble/pallas_call | solution.py:465
  28.4 2.1 %collective-permute-done.8 = f32[8,128]{1,0:T(8,128)S(1)} collective-permute-done((f32[8,128]{1,0:T(8,128)S(1)}, f32[8,128]{1,0:T(8,128)S(1)}, u32[]{:S(2)}, u32[]{:S(2)}) %collective-permute-start.8) | collective-permute-done | bytes 4128 | tf_op jit(solution)/shard_map/ppermute | solution.py:449
  30.6 0.4 %expand.1 = (bf16[96,1024]{1,0:T(8,128)(2,1)S(1)}, s32[1,1024]{1,0:T(1,128)S(1)}) custom-call(s32[256,3]{1,0:T(8,128)S(1)} %get-tuple-element.29.where_ref, f32[2,128]{1,0:T(2,128)S(1)} %ensemble.4.after_ref), custom_call_target="tpu_custom_call" | custom-call | flops 100000000 | bytes 1000000 | tf_op jit(solution)/shard_map/expand/pallas_call | solution.py:521
  31.1 0.7 %collective-permute-done.9.far_ref = f32[24,128]{1,0:T(8,128)S(1)} collective-permute-done((f32[24,128]{1,0:T(8,128)S(1)}, f32[24,128]{1,0:T(8,128)S(1)}, u32[]{:S(2)}, u32[]{:S(2)}) %collective-permute-start.9) | collective-permute-done | bytes 12320 | tf_op jit(solution)/shard_map/ppermute | solution.py:388
  31.8 0.9 %finish.1 = f32[1,1024]{1,0:T(1,128)} custom-call(bf16[96,1024]{1,0:T(8,128)(2,1)S(1)} %get-tuple-element.48.line_ref, s32[1,1024]{1,0:T(1,128)S(1)} %get-tuple-element.49.lane_ref, f32[24,128]{1,0:T(8,128)S(1)} %concatenate.8.near_ref, f32[24,128]{1,0:T(8,128)S(1)} %collective-permute-done.9.far_ref), custom_call_target="tpu_custom_call" | custom-call | flops 1000000 | bytes 1000000 | tf_op jit(solution)/shard_map/finish/pallas_call | solution.py:531
  (36 shorter events, 0.4 us)
Async XLA Ops:
  0.0 2.6 %collective-permute-start = (bf16[3,512,256]{2,1,0:T(8,128)(2,1)}, bf16[3,512,256]{2,1,0:T(8,128)(2,1)S(1)}, u32[]{:S(2)}, u32[]{:S(2)}) collective-permute-start(bf16[3,512,256]{2,1,0:T(8,128)(2,1)} %q0_ref.3), channel_id=1, source_target_pairs={{0,1},{1,0},{2,3},{3,2},{4,5},{5,4},{6,7},{7,6},{8,9},{9,8},{10,11... | collective-permute-start | bytes 2359304 | tf_op jit(solution)/shard_map/ppermute | solution.py:388
  0.5 2.6 %copy-start = (bf16[2,512,1024]{2,1,0:T(8,128)(2,1)S(1)}, bf16[2,512,1024]{2,1,0:T(8,128)(2,1)}, u32[]{:S(2)}) copy-start(bf16[2,512,1024]{2,1,0:T(8,128)(2,1)} %w_ref.7) | copy-start | bytes 6291460
  0.5 2.6 %copy-start.3 = (f32[2,1024]{1,0:T(2,128)S(1)}, f32[2,1024]{1,0:T(2,128)}, u32[]{:S(2)}) copy-start(f32[2,1024]{1,0:T(2,128)} %bias_ref.7) | copy-start | bytes 24580
  0.5 2.6 %copy-start.4 = (bf16[2,1024]{1,0:T(2,128)(2,1)S(1)}, bf16[2,1024]{1,0:T(2,128)(2,1)}, u32[]{:S(2)}) copy-start(bf16[2,1024]{1,0:T(2,128)(2,1)} %out_ref.7) | copy-start | bytes 12292
  0.5 2.6 %copy-start.7 = (f32[1,512]{1,0:T(1,128)S(1)}, f32[1,512]{1,0:T(1,128)}, u32[]{:S(2)}) copy-start(f32[1,512]{1,0:T(1,128)} %upb_ref.1) | copy-start | bytes 6148
  0.5 2.6 %copy-start.8 = (f32[1,512]{1,0:T(1,128)S(1)}, f32[1,512]{1,0:T(1,128)}, u32[]{:S(2)}) copy-start(f32[1,512]{1,0:T(1,128)} %head_ref.1) | copy-start | bytes 6148
  3.0 4.4 %copy-start.2 = (bf16[3,512,256]{2,1,0:T(8,128)(2,1)S(1)}, bf16[3,512,256]{2,1,0:T(8,128)(2,1)}, u32[]{:S(2)}) copy-start(bf16[3,512,256]{2,1,0:T(8,128)(2,1)} %q0_ref.3) | copy-start | bytes 2359300
  3.0 4.4 %copy-start.5 = (f32[4,512]{1,0:T(4,128)S(1)}, f32[4,512]{1,0:T(4,128)}, u32[]{:S(2)}) copy-start(f32[4,512]{1,0:T(4,128)} %scale_ref.1) | copy-start | bytes 24580
  3.1 4.4 %copy-start.6 = (f32[4,512]{1,0:T(4,128)S(1)}, f32[4,512]{1,0:T(4,128)}, u32[]{:S(2)}) copy-start(f32[4,512]{1,0:T(4,128)} %shift_ref.1) | copy-start | bytes 24580
  3.1 4.4 %copy-start.9 = (f32[512]{0:T(512)S(1)}, f32[512]{0:T(512)}, u32[]{:S(2)}) copy-start(f32[512]{0:T(512)} %param.29) | copy-start | bytes 6148
  3.1 4.4 %copy-start.10 = (f32[512]{0:T(512)S(1)}, f32[512]{0:T(512)}, u32[]{:S(2)}) copy-start(f32[512]{0:T(512)} %param.30) | copy-start | bytes 6148
  3.1 4.4 %copy-start.11 = (f32[512]{0:T(512)S(1)}, f32[512]{0:T(512)}, u32[]{:S(2)}) copy-start(f32[512]{0:T(512)} %param.26) | copy-start | bytes 6148
  3.1 4.4 %copy-start.12 = (f32[512]{0:T(512)S(1)}, f32[512]{0:T(512)}, u32[]{:S(2)}) copy-start(f32[512]{0:T(512)} %param.33) | copy-start | bytes 6148
  4.5 3.8 %collective-permute-start.1 = (bf16[1040,512]{1,0:T(8,128)(2,1)S(1)}, bf16[1040,512]{1,0:T(8,128)(2,1)S(1)}, u32[]{:S(2)}, u32[]{:S(2)}) collective-permute-start(bf16[1040,512]{1,0:T(8,128)(2,1)S(1)} %get-tuple-element.35.fw0_ref.refs_1_), channel_id=1, source_target_pairs={{0,1},{1,0},{2,3},{3,2},{4,5},{5,4},{6,7},{7,6},{8,9},{9,8},{10,11... | collective-permute-start | bytes 3194888 | tf_op jit(solution)/shard_map/ppermute | solution.py:388
  4.5 16.8 %collective-permute-start.6 = (bf16[528,512]{1,0:T(8,128)(2,1)S(1)}, bf16[528,512]{1,0:T(8,128)(2,1)S(1)}, u32[]{:S(2)}, u32[]{:S(2)}) collective-permute-start(bf16[528,512]{1,0:T(8,128)(2,1)S(1)} %get-tuple-element.47), channel_id=1, source_target_pairs={{0,2},{2,0},{4,6},{6,4},{8,10},{10,8},{12,14},{14,12},{1,3},{3,1},... | collective-permute-start | bytes 1622024 | tf_op jit(solution)/shard_map/ppermute | solution.py:424
  8.3 6.6 %copy-start.1 = (bf16[1024,512]{1,0:T(8,128)(2,1)S(1)}, bf16[1024,512]{1,0:T(8,128)(2,1)}, u32[]{:S(2)}) copy-start(bf16[1024,512]{1,0:T(8,128)(2,1)} %feat_ref.5) | copy-start | bytes 3145732
  10.4 6.8 %collective-permute-start.2 = (bf16[64,512]{1,0:T(8,128)(2,1)S(1)}, bf16[64,512]{1,0:T(8,128)(2,1)S(1)}, u32[]{:S(2)}, u32[]{:S(2)}) collective-permute-start(bf16[64,512]{1,0:T(8,128)(2,1)S(1)} %get-tuple-element.38), channel_id=1, source_target_pairs={{0,12},{2,14},{4,8},{6,10},{8,4},{10,6},{12,0},{14,2},{1,13},{3,15... | collective-permute-start | bytes 196616 | tf_op jit(solution)/shard_map/ppermute | solution.py:449
  14.1 6.0 %collective-permute-start.3 = (bf16[64,512]{1,0:T(8,128)(2,1)S(1)}, bf16[64,512]{1,0:T(8,128)(2,1)S(1)}, u32[]{:S(2)}, u32[]{:S(2)}) collective-permute-start(bf16[64,512]{1,0:T(8,128)(2,1)S(1)} %get-tuple-element.39), channel_id=1, source_target_pairs={{0,8},{2,10},{4,12},{6,14},{8,0},{10,2},{12,4},{14,6},{1,9},{3,11}... | collective-permute-start | bytes 196616 | tf_op jit(solution)/shard_map/ppermute | solution.py:449
  14.1 6.0 %collective-permute-start.4 = (bf16[64,512]{1,0:T(8,128)(2,1)S(1)}, bf16[64,512]{1,0:T(8,128)(2,1)S(1)}, u32[]{:S(2)}, u32[]{:S(2)}) collective-permute-start(bf16[64,512]{1,0:T(8,128)(2,1)S(1)} %get-tuple-element.40), channel_id=1, source_target_pairs={{0,4},{2,6},{4,0},{6,2},{8,12},{10,14},{12,8},{14,10},{1,5},{3,7},... | collective-permute-start | bytes 196616 | tf_op jit(solution)/shard_map/ppermute | solution.py:449
  20.5 1.4 %collective-permute-start.5 = (bf16[128,512]{1,0:T(8,128)(2,1)S(1)}, bf16[128,512]{1,0:T(8,128)(2,1)S(1)}, u32[]{:S(2)}, u32[]{:S(2)}) collective-permute-start(bf16[128,512]{1,0:T(8,128)(2,1)S(1)} %get-tuple-element.46.mine_ref), channel_id=1, source_target_pairs={{0,1},{1,0},{2,3},{3,2},{4,5},{5,4},{6,7},{7,6},{8,9},{9,8},{10,11... | collective-permute-start | bytes 393224 | tf_op jit(solution)/shard_map/ppermute | solution.py:388
  22.3 3.7 %collective-permute-start.7 = (f32[4,128]{1,0:T(4,128)S(1)}, f32[4,128]{1,0:T(4,128)S(1)}, u32[]{:S(2)}, u32[]{:S(2)}) collective-permute-start(f32[4,128]{1,0:T(4,128)S(1)} %far_score.1.after_ref), channel_id=1, source_target_pairs={{0,4},{2,6},{4,0},{6,2},{8,12},{10,14},{12,8},{14,10},{1,5},{3,7},... | collective-permute-start | bytes 6152 | tf_op jit(solution)/shard_map/ppermute | solution.py:449
  26.0 4.5 %collective-permute-start.8 = (f32[8,128]{1,0:T(8,128)S(1)}, f32[8,128]{1,0:T(8,128)S(1)}, u32[]{:S(2)}, u32[]{:S(2)}) collective-permute-start(f32[8,128]{1,0:T(8,128)S(1)} %pad_maximum_fusion), channel_id=1, source_target_pairs={{0,8},{2,10},{4,12},{6,14},{8,0},{10,2},{12,4},{14,6},{1,9},{3,11}... | collective-permute-start | bytes 12296 | tf_op jit(solution)/shard_map/ppermute | solution.py:449
  30.5 1.2 %collective-permute-start.9 = (f32[24,128]{1,0:T(8,128)S(1)}, f32[24,128]{1,0:T(8,128)S(1)}, u32[]{:S(2)}, u32[]{:S(2)}) collective-permute-start(f32[24,128]{1,0:T(8,128)S(1)} %concatenate.8.near_ref), channel_id=1, source_target_pairs={{0,1},{1,0},{2,3},{3,2},{4,5},{5,4},{6,7},{7,6},{8,9},{9,8},{10,11... | collective-permute-start | bytes 36872 | tf_op jit(solution)/shard_map/ppermute | solution.py:388

commit v4 on v1

--- a/solution.py
+++ b/solution.py
@@ -140,7 +140,7 @@
 
 
 def constants_kernel(
-    cls_ref, gain_ref, scale_ref, shift_ref, fbias_ref, fgain_ref, q0_ref, q1_ref, index_ref,
+    cls_ref, gain_ref, scale_ref, shift_ref, fbias_ref, fgain_ref, q0_ref, q1_ref, index_ref, after_ref,
     table_ref, where_ref, place_ref,
 ):
     count = index_ref.shape[1]
@@ -420,12 +420,12 @@
     table, where, place = pl.pallas_call(
         constants_kernel,
         out_shape=[shape((TABLE, width), F32), shape((count, 3), jnp.int32), shape((1, dealt), jnp.int32)],
-        in_specs=[VMEM] * len(ins),
+        in_specs=[VMEM] * len(ins) + [ANY],
         out_specs=[VMEM] * 3,
         compiler_params=params(16),
         cost_estimate=cost(10**8, 2 * 10**6),
         name="constants",
-    )(*ins)
+    )(*ins, other_both)
 
     local = qkv_weight.shape[2]
     sent = pl.pallas_call(

time: 32.4 us -> 33.2 us (1.025)
  waiting for transfers between devices: 7.15 us -> 7.59 us
  starting transfers between devices: 11 us -> 11.4 us
    ppermute x5, waiting for transfers between devices: 5.86 us -> 6.29 us  [across(): return lax.ppermute(x, 'rows', [(i, i ^ 2 * k) for i in range(n)])]
    ppermute x5, starting transfers between devices: 7.04 us -> 7.44 us  [across(): return lax.ppermute(x, 'rows', [(i, i ^ 2 * k) for i in range(n)])]
  transfers between devices with their start and end apart: 11 -> 11, of which waited for: 5 -> 5; matrix products, arithmetic and copies ran while one was open for 0% -> 0% of each run, Pallas kernels for 38% -> 37%
where the time goes in v4:
time: 33.2 us; the launch traced here: 33.1 us
  Pallas kernels  13.7 us (41%)
  starting transfers between devices  11.4 us (34%)
  waiting for transfers between devices  7.59 us (23%)
    ppermute x5, starting transfers between devices, across(): return lax.ppermute(x, 'rows', [(i, i ^ 2 * k) for i in range(n)])  7.44 us
    ppermute x5, waiting for transfers between devices, across(): return lax.ppermute(x, 'rows', [(i, i ^ 2 * k) for i in range(n)])  6.29 us
    pallas_call x3, Pallas kernels, ensemble(): pl.pallas_call(functools.partial(ensemble_kernel, first, number, tile), o...  4.66 us
    ppermute x1, starting transfers between devices, per_device(): next_segment = lax.ppermute(segment, 'rows', [(i, i ^ 1) for i in range(n)])  2.76 us
    pallas_call x1, Pallas kernels, per_device(): pl.pallas_call(functools.partial(attend_kernel, members), out_shape=[shap...  2.11 us
    pallas_call x1, Pallas kernels, per_device(): pl.pallas_call(functools.partial(route_kernel, n, half, relative), out_sh...  1.91 us
    pallas_call x1, Pallas kernels, per_device(): pl.pallas_call(predict_kernel, out_shape=[shape((8, dealt), F32), shape(s...  1.34 us
    ppermute x5, waiting for transfers between devices, swap(): return lax.ppermute(x, 'member', [(0, 1), (1, 0)])  1.3 us
  transfers between devices with their start and end apart: 11, of which 5 were waited for; matrix products, arithmetic and copies ran while one was open for 0% of the time, Pallas kernels for 37%

profile of v4, /device:TPU:0, one launch (start us, length us, event | category | flops | bytes accessed | tf_op | source)
XLA Modules:
  0.0 33.1 jit_solution(2415124120188789108)
XLA Ops:
  0.0 0.5 %collective-permute-start = (bf16[3,512,256]{2,1,0:T(8,128)(2,1)}, bf16[3,512,256]{2,1,0:T(8,128)(2,1)S(1)}, u32[]{:S(2)}, u32[]{:S(2)}) collective-permute-start(bf16[3,512,256]{2,1,0:T(8,128)(2,1)} %q0_ref.3), channel_id=1, source_target_pairs={{0,1},{1,0},{2,3},{3,2},{4,5},{5,4},{6,7},{7,6},{8,9},{9,8},{10,11... | collective-permute-start | bytes 2359304 | tf_op jit(solution)/shard_map/ppermute | solution.py:380
  0.5 1.9 %route.1 = (s32[8,256]{1,0:T(8,128)S(1)}, bf16[256,512]{1,0:T(8,128)(2,1)S(1)}, bf16[512,512]{1,0:T(8,128)(2,1)S(1)}, bf16[528,512]{1,0:T(8,128)(2,1)S(1)}, bf16[512,512]{1,0:T(8,128)(2,1)S(1)}) custom-call(s32[1,256]{1,0:T(1,128)} %esc_hbm.1, s32[1,256]{1,0:T(1,128)} %bitcast.10, bf16[1024,512]{1,0:T(8,128)(2,1)} %feat_ref.5, ...), custom_call_target="tpu_custom_call" | custom-call | flops 268435456 | bytes 3000000 | tf_op jit(solution)/shard_map/route/pallas_call | solution.py:393
  2.6 1.3 %predict.1 = (f32[8,128]{1,0:T(8,128)S(1)}, bf16[528,512]{1,0:T(8,128)(2,1)S(1)}) custom-call(bf16[256,512]{1,0:T(8,128)(2,1)S(1)} %get-tuple-element.32.rows_ref, bf16[2,512,1024]{2,1,0:T(8,128)(2,1)S(1)} %copy-done, f32[2,1024]{1,0:T(2,128)S(1)} %copy-done.3, bf16[2,1024]{1,0:T(2,128)(2,1)S(1)} %copy-done.4, ...), custom_call_target="tpu_custom_call", output_to_operand_aliasing={{1}: (7, {})} | custom-call | flops 536870912 | bytes 3000000 | tf_op jit(solution)/shard_map/predict/pallas_call | solution.py:405
  3.9 0.3 collective-permute-start.2
  4.5 2.8 %collective-permute-start.7 = (bf16[528,512]{1,0:T(8,128)(2,1)S(1)}, bf16[528,512]{1,0:T(8,128)(2,1)S(1)}, u32[]{:S(2)}, u32[]{:S(2)}) collective-permute-start(bf16[528,512]{1,0:T(8,128)(2,1)S(1)} %get-tuple-element.36.refs_3_), channel_id=1, source_target_pairs={{0,2},{2,0},{4,6},{6,4},{8,10},{10,8},{12,14},{14,12},{1,3},{3,1},... | collective-permute-start | bytes 1622024 | tf_op jit(solution)/shard_map/ppermute | solution.py:416
  7.3 0.8 %constants.1 = (f32[40,512]{1,0:T(8,128)S(1)}, s32[256,3]{1,0:T(8,128)S(1)}, s32[1,128]{1,0:T(1,128)S(1)}) custom-call(f32[1,512]{1,0:T(1,128)S(1)} %bitcast.6, f32[1,512]{1,0:T(1,128)S(1)} %bitcast.7, f32[4,512]{1,0:T(4,128)S(1)} %copy-done.5, f32[4,512]{1,0:T(4,128)S(1)} %copy-done.6, f32[1,512]{1,0:T(1,128)S(1)} %bitcast.8, f32[1,512]{1,0:T(1,128)S(1)} %bitcast.9, ...), custom_call_target="tpu_custom_call" | custom-call | flops 100000000 | bytes 2000000 | tf_op jit(solution)/shard_map/constants/pallas_call | solution.py:420
  8.1 2.1 %attend.1 = (bf16[64,512]{1,0:T(8,128)(2,1)S(1)}, bf16[64,512]{1,0:T(8,128)(2,1)S(1)}, bf16[64,512]{1,0:T(8,128)(2,1)S(1)}, bf16[64,512]{1,0:T(8,128)(2,1)S(1)}) custom-call(bf16[256,512]{1,0:T(8,128)(2,1)S(1)} %get-tuple-element.32.rows_ref, f32[8,128]{1,0:T(8,128)S(1)} %get-tuple-element.35.near_ref, ...), custom_call_target="tpu_custom_call" | custom-call | flops 1000000000 | bytes 2000000 | tf_op jit(solution)/shard_map/attend/pallas_call | solution.py:431
  10.2 4.4 %collective-permute-start.3 = (bf16[64,512]{1,0:T(8,128)(2,1)S(1)}, bf16[64,512]{1,0:T(8,128)(2,1)S(1)}, u32[]{:S(2)}, u32[]{:S(2)}) collective-permute-start(bf16[64,512]{1,0:T(8,128)(2,1)S(1)} %get-tuple-element.39), channel_id=1, source_target_pairs={{0,12},{2,14},{4,8},{6,10},{8,4},{10,6},{12,0},{14,2},{1,13},{3,15... | collective-permute-start | bytes 196616 | tf_op jit(solution)/shard_map/ppermute | solution.py:442
  14.5 0.6 %collective-permute-start.5 = (bf16[64,512]{1,0:T(8,128)(2,1)S(1)}, bf16[64,512]{1,0:T(8,128)(2,1)S(1)}, u32[]{:S(2)}, u32[]{:S(2)}) collective-permute-start(bf16[64,512]{1,0:T(8,128)(2,1)S(1)} %get-tuple-element.41), channel_id=1, source_target_pairs={{0,4},{2,6},{4,0},{6,2},{8,12},{10,14},{12,8},{14,10},{1,5},{3,7},... | collective-permute-start | bytes 196616 | tf_op jit(solution)/shard_map/ppermute | solution.py:442
  15.2 2.4 %ensemble.3 = (f32[4,128]{1,0:T(4,128)S(1)}, f32[40,512]{1,0:T(8,128)S(1)}, bf16[512,512]{1,0:T(8,128)(2,1)S(1)}, bf16[512,512]{1,0:T(8,128)(2,1)S(1)}, bf16[528...) custom-call(bf16[1024,512]{1,0:T(8,128)(2,1)S(1)} %copy-done.1, bf16[2,512,1024]{2,1,0:T(8,128)(2,1)S(1)} %copy-done, ...), custom_call_target="tpu_custom_call" | custom-call | flops 1073741824 | bytes 1000000 | tf_op jit(solution)/shard_map/ensemble/pallas_call | solution.py:458
  17.6 2.8 %collective-permute-done.4.refs_1_ = bf16[64,512]{1,0:T(8,128)(2,1)S(1)} collective-permute-done((bf16[64,512]{1,0:T(8,128)(2,1)S(1)}, bf16[64,512]{1,0:T(8,128)(2,1)S(1)}, u32[]{:S(2)}, u32[]{:S(2)}) %collective-permute-start.4) | collective-permute-done | bytes 65568 | tf_op jit(solution)/shard_map/ppermute | solution.py:442
  20.4 0.4 %arrive.1 = (f32[128,512]{1,0:T(8,128)S(1)}, bf16[128,512]{1,0:T(8,128)(2,1)S(1)}) custom-call(bf16[64,512]{1,0:T(8,128)(2,1)S(1)} %collective-permute-done.3.refs_0_, bf16[64,512]{1,0:T(8,128)(2,1)S(1)} %collective-permute-done.4.refs_1_, bf16[64,512]{1,0:T(8,128)(2,1)S(1)} %collective-permute-done.5.refs_2_, ...), custom_call_target="tpu_custom_call" | custom-call | flops 200000000 | bytes 2000000 | tf_op jit(solution)/shard_map/arrive/pallas_call | solution.py:474
  20.9 0.8 %near_score.1.near_ref = f32[128,1]{1,0:T(8,128)S(1)} custom-call(bf16[64,512]{1,0:T(8,128)(2,1)S(1)} %collective-permute-done.3.refs_0_, bf16[64,512]{1,0:T(8,128)(2,1)S(1)} %collective-permute-done.4.refs_1_, bf16[64,512]{1,0:T(8,128)(2,1)S(1)} %collective-permute-done.5.refs_2_, bf16[64,512]{1,0:T(8,128)(2,1)S(1)} %get-tuple-element.42.after_ref.refs_3_, ...), custom_call_target="tpu_custom_call" | custom-call | flops 500000000 | bytes 2000000 | tf_op jit(solution)/shard_map/near_score/pallas_call | solution.py:484
  21.7 0.6 %collective-permute-done.6.other_ref = bf16[128,512]{1,0:T(8,128)(2,1)S(1)} collective-permute-done((bf16[128,512]{1,0:T(8,128)(2,1)S(1)}, bf16[128,512]{1,0:T(8,128)(2,1)S(1)}, u32[]{:S(2)}, u32[]{:S(2)}) %collective-permute-start.6) | collective-permute-done | bytes 131104 | tf_op jit(solution)/shard_map/ppermute | solution.py:380
  22.3 0.4 %far_score.1.after_ref = f32[4,128]{1,0:T(4,128)S(1)} custom-call(f32[128,1]{1,0:T(8,128)S(1)} %near_score.1.near_ref, f32[128,512]{1,0:T(8,128)S(1)} %get-tuple-element.48.state_ref, bf16[128,512]{1,0:T(8,128)(2,1)S(1)} %get-tuple-element.49.mine_ref, bf16[128,512]{1,0:T(8,128)(2,1)S(1)} %collective-permute-done.6.other_ref, ...), custom_call_target="tpu_custom_call" | custom-call | flops 200000000 | bytes 1000000 | tf_op jit(solution)/shard_map/far_score/pallas_call | solution.py:493
  22.7 1.1 %collective-permute-start.8 = (f32[4,128]{1,0:T(4,128)S(1)}, f32[4,128]{1,0:T(4,128)S(1)}, u32[]{:S(2)}, u32[]{:S(2)}) collective-permute-start(f32[4,128]{1,0:T(4,128)S(1)} %far_score.1.after_ref), channel_id=1, source_target_pairs={{0,4},{2,6},{4,0},{6,2},{8,12},{10,14},{12,8},{14,10},{1,5},{3,7},... | collective-permute-start | bytes 6152 | tf_op jit(solution)/shard_map/ppermute | solution.py:442
  23.8 1.1 %ensemble.4.after_ref = f32[2,128]{1,0:T(2,128)S(1)} custom-call(bf16[1024,512]{1,0:T(8,128)(2,1)S(1)} %copy-done.1, bf16[2,512,1024]{2,1,0:T(8,128)(2,1)S(1)} %copy-done, f32[2,1024]{1,0:T(2,128)S(1)} %copy-done.3, bf16[2,1024]{1,0:T(2,128)(2,1)S(1)} %copy-done.4, f32[4,128]{1,0:T(4,128)S(1)} %far_score.1.after_ref), custom_call_target="tpu_custom_call" | custom-call | flops 536870912 | bytes 1000000 | tf_op jit(solution)/shard_map/ensemble/pallas_call | solution.py:458
  25.0 1.4 %collective-permute-done.8 = f32[4,128]{1,0:T(4,128)S(1)} collective-permute-done((f32[4,128]{1,0:T(4,128)S(1)}, f32[4,128]{1,0:T(4,128)S(1)}, u32[]{:S(2)}, u32[]{:S(2)}) %collective-permute-start.8) | collective-permute-done | bytes 2080 | tf_op jit(solution)/shard_map/ppermute | solution.py:442
  26.3 1.3 %collective-permute-start.9 = (f32[8,128]{1,0:T(8,128)S(1)}, f32[8,128]{1,0:T(8,128)S(1)}, u32[]{:S(2)}, u32[]{:S(2)}) collective-permute-start(f32[8,128]{1,0:T(8,128)S(1)} %pad_maximum_fusion), channel_id=1, source_target_pairs={{0,8},{2,10},{4,12},{6,14},{8,0},{10,2},{12,4},{14,6},{1,9},{3,11}... | collective-permute-start | bytes 12296 | tf_op jit(solution)/shard_map/ppermute | solution.py:442
  27.6 1.1 %ensemble.5 = f32[2,128]{1,0:T(2,128)S(1)} custom-call(bf16[1024,512]{1,0:T(8,128)(2,1)S(1)} %copy-done.1, bf16[2,512,1024]{2,1,0:T(8,128)(2,1)S(1)} %copy-done, f32[2,1024]{1,0:T(2,128)S(1)} %copy-done.3, bf16[2,1024]{1,0:T(2,128)(2,1)S(1)} %copy-done.4, f32[4,128]{1,0:T(4,128)S(1)} %far_score.1.after_ref), custom_call_target="tpu_custom_call" | custom-call | flops 536870912 | bytes 1000000 | tf_op jit(solution)/shard_map/ensemble/pallas_call | solution.py:458
  28.8 2.1 %collective-permute-done.9 = f32[8,128]{1,0:T(8,128)S(1)} collective-permute-done((f32[8,128]{1,0:T(8,128)S(1)}, f32[8,128]{1,0:T(8,128)S(1)}, u32[]{:S(2)}, u32[]{:S(2)}) %collective-permute-start.9) | collective-permute-done | bytes 4128 | tf_op jit(solution)/shard_map/ppermute | solution.py:442
  31.0 0.4 %expand.1 = (bf16[96,1024]{1,0:T(8,128)(2,1)S(1)}, s32[1,1024]{1,0:T(1,128)S(1)}) custom-call(s32[256,3]{1,0:T(8,128)S(1)} %get-tuple-element.31.where_ref, f32[2,128]{1,0:T(2,128)S(1)} %ensemble.4.after_ref), custom_call_target="tpu_custom_call" | custom-call | flops 100000000 | bytes 1000000 | tf_op jit(solution)/shard_map/expand/pallas_call | solution.py:515
  31.4 0.7 %collective-permute-done.10.far_ref = f32[24,128]{1,0:T(8,128)S(1)} collective-permute-done((f32[24,128]{1,0:T(8,128)S(1)}, f32[24,128]{1,0:T(8,128)S(1)}, u32[]{:S(2)}, u32[]{:S(2)}) %collective-permute-start.10) | collective-permute-done | bytes 12320 | tf_op jit(solution)/shard_map/ppermute | solution.py:380
  32.1 0.9 %finish.1 = f32[1,1024]{1,0:T(1,128)} custom-call(bf16[96,1024]{1,0:T(8,128)(2,1)S(1)} %get-tuple-element.50.line_ref, s32[1,1024]{1,0:T(1,128)S(1)} %get-tuple-element.51.lane_ref, f32[24,128]{1,0:T(8,128)S(1)} %concatenate.8.near_ref, f32[24,128]{1,0:T(8,128)S(1)} %collective-permute-done.10.far_ref), custom_call_target="tpu_custom_call" | custom-call | flops 1000000 | bytes 1000000 | tf_op jit(solution)/shard_map/finish/pallas_call | solution.py:525
  (38 shorter events, 0.5 us)
Async XLA Ops:
  0.0 2.6 %copy-start = (bf16[2,512,1024]{2,1,0:T(8,128)(2,1)S(1)}, bf16[2,512,1024]{2,1,0:T(8,128)(2,1)}, u32[]{:S(2)}) copy-start(bf16[2,512,1024]{2,1,0:T(8,128)(2,1)} %w_ref.7) | copy-start | bytes 6291460
  0.0 2.6 %copy-start.3 = (f32[2,1024]{1,0:T(2,128)S(1)}, f32[2,1024]{1,0:T(2,128)}, u32[]{:S(2)}) copy-start(f32[2,1024]{1,0:T(2,128)} %bias_ref.7) | copy-start | bytes 24580
  0.0 2.6 %copy-start.4 = (bf16[2,1024]{1,0:T(2,128)(2,1)S(1)}, bf16[2,1024]{1,0:T(2,128)(2,1)}, u32[]{:S(2)}) copy-start(bf16[2,1024]{1,0:T(2,128)(2,1)} %out_ref.7) | copy-start | bytes 12292
  0.0 2.6 %copy-start.7 = (f32[1,512]{1,0:T(1,128)S(1)}, f32[1,512]{1,0:T(1,128)}, u32[]{:S(2)}) copy-start(f32[1,512]{1,0:T(1,128)} %upb_ref.1) | copy-start | bytes 6148
  0.0 2.6 %copy-start.8 = (f32[1,512]{1,0:T(1,128)S(1)}, f32[1,512]{1,0:T(1,128)}, u32[]{:S(2)}) copy-start(f32[1,512]{1,0:T(1,128)} %head_ref.1) | copy-start | bytes 6148
  0.0 7.2 %collective-permute-start = (bf16[3,512,256]{2,1,0:T(8,128)(2,1)}, bf16[3,512,256]{2,1,0:T(8,128)(2,1)S(1)}, u32[]{:S(2)}, u32[]{:S(2)}) collective-permute-start(bf16[3,512,256]{2,1,0:T(8,128)(2,1)} %q0_ref.3), channel_id=1, source_target_pairs={{0,1},{1,0},{2,3},{3,2},{4,5},{5,4},{6,7},{7,6},{8,9},{9,8},{10,11... | collective-permute-start | bytes 2359304 | tf_op jit(solution)/shard_map/ppermute | solution.py:380
  2.5 4.8 %copy-start.2 = (bf16[3,512,256]{2,1,0:T(8,128)(2,1)S(1)}, bf16[3,512,256]{2,1,0:T(8,128)(2,1)}, u32[]{:S(2)}) copy-start(bf16[3,512,256]{2,1,0:T(8,128)(2,1)} %q0_ref.3) | copy-start | bytes 2359300
  2.5 4.8 %copy-start.5 = (f32[4,512]{1,0:T(4,128)S(1)}, f32[4,512]{1,0:T(4,128)}, u32[]{:S(2)}) copy-start(f32[4,512]{1,0:T(4,128)} %scale_ref.1) | copy-start | bytes 24580
  2.5 4.8 %copy-start.6 = (f32[4,512]{1,0:T(4,128)S(1)}, f32[4,512]{1,0:T(4,128)}, u32[]{:S(2)}) copy-start(f32[4,512]{1,0:T(4,128)} %shift_ref.1) | copy-start | bytes 24580
  2.5 4.7 %copy-start.9 = (f32[512]{0:T(512)S(1)}, f32[512]{0:T(512)}, u32[]{:S(2)}) copy-start(f32[512]{0:T(512)} %param.29) | copy-start | bytes 6148
  2.5 4.7 %copy-start.10 = (f32[512]{0:T(512)S(1)}, f32[512]{0:T(512)}, u32[]{:S(2)}) copy-start(f32[512]{0:T(512)} %param.30) | copy-start | bytes 6148
  2.5 4.7 %copy-start.11 = (f32[512]{0:T(512)S(1)}, f32[512]{0:T(512)}, u32[]{:S(2)}) copy-start(f32[512]{0:T(512)} %param.26) | copy-start | bytes 6148
  2.5 4.7 %copy-start.12 = (f32[512]{0:T(512)S(1)}, f32[512]{0:T(512)}, u32[]{:S(2)}) copy-start(f32[512]{0:T(512)} %param.33) | copy-start | bytes 6148
  3.9 4.1 %collective-permute-start.2 = (bf16[528,512]{1,0:T(8,128)(2,1)S(1)}, bf16[528,512]{1,0:T(8,128)(2,1)S(1)}, u32[]{:S(2)}, u32[]{:S(2)}) collective-permute-start(bf16[528,512]{1,0:T(8,128)(2,1)S(1)} %get-tuple-element.36.refs_3_), channel_id=1, source_target_pairs={{0,1},{1,0},{2,3},{3,2},{4,5},{5,4},{6,7},{7,6},{8,9},{9,8},{10,11... | collective-permute-start | bytes 1622024 | tf_op jit(solution)/shard_map/ppermute | solution.py:380
  4.2 3.0 %collective-permute-start.1 = (bf16[512,512]{1,0:T(8,128)(2,1)S(1)}, bf16[512,512]{1,0:T(8,128)(2,1)S(1)}, u32[]{:S(2)}, u32[]{:S(2)}) collective-permute-start(bf16[512,512]{1,0:T(8,128)(2,1)S(1)} %get-tuple-element.30.fw0_ref.refs_1_), channel_id=1, source_target_pairs={{0,1},{1,0},{2,3},{3,2},{4,5},{5,4},{6,7},{7,6},{8,9},{9,8},{10,11... | collective-permute-start | bytes 1572872 | tf_op jit(solution)/shard_map/ppermute | solution.py:380
  4.5 17.2 %collective-permute-start.7 = (bf16[528,512]{1,0:T(8,128)(2,1)S(1)}, bf16[528,512]{1,0:T(8,128)(2,1)S(1)}, u32[]{:S(2)}, u32[]{:S(2)}) collective-permute-start(bf16[528,512]{1,0:T(8,128)(2,1)S(1)} %get-tuple-element.36.refs_3_), channel_id=1, source_target_pairs={{0,2},{2,0},{4,6},{6,4},{8,10},{10,8},{12,14},{14,12},{1,3},{3,1},... | collective-permute-start | bytes 1622024 | tf_op jit(solution)/shard_map/ppermute | solution.py:416
  8.0 7.1 %copy-start.1 = (bf16[1024,512]{1,0:T(8,128)(2,1)S(1)}, bf16[1024,512]{1,0:T(8,128)(2,1)}, u32[]{:S(2)}) copy-start(bf16[1024,512]{1,0:T(8,128)(2,1)} %feat_ref.5) | copy-start | bytes 3145732
  10.2 7.4 %collective-permute-start.3 = (bf16[64,512]{1,0:T(8,128)(2,1)S(1)}, bf16[64,512]{1,0:T(8,128)(2,1)S(1)}, u32[]{:S(2)}, u32[]{:S(2)}) collective-permute-start(bf16[64,512]{1,0:T(8,128)(2,1)S(1)} %get-tuple-element.39), channel_id=1, source_target_pairs={{0,12},{2,14},{4,8},{6,10},{8,4},{10,6},{12,0},{14,2},{1,13},{3,15... | collective-permute-start | bytes 196616 | tf_op jit(solution)/shard_map/ppermute | solution.py:442
  14.5 5.9 %collective-permute-start.4 = (bf16[64,512]{1,0:T(8,128)(2,1)S(1)}, bf16[64,512]{1,0:T(8,128)(2,1)S(1)}, u32[]{:S(2)}, u32[]{:S(2)}) collective-permute-start(bf16[64,512]{1,0:T(8,128)(2,1)S(1)} %get-tuple-element.40), channel_id=1, source_target_pairs={{0,8},{2,10},{4,12},{6,14},{8,0},{10,2},{12,4},{14,6},{1,9},{3,11}... | collective-permute-start | bytes 196616 | tf_op jit(solution)/shard_map/ppermute | solution.py:442
  14.5 5.9 %collective-permute-start.5 = (bf16[64,512]{1,0:T(8,128)(2,1)S(1)}, bf16[64,512]{1,0:T(8,128)(2,1)S(1)}, u32[]{:S(2)}, u32[]{:S(2)}) collective-permute-start(bf16[64,512]{1,0:T(8,128)(2,1)S(1)} %get-tuple-element.41), channel_id=1, source_target_pairs={{0,4},{2,6},{4,0},{6,2},{8,12},{10,14},{12,8},{14,10},{1,5},{3,7},... | collective-permute-start | bytes 196616 | tf_op jit(solution)/shard_map/ppermute | solution.py:442
  20.8 1.4 %collective-permute-start.6 = (bf16[128,512]{1,0:T(8,128)(2,1)S(1)}, bf16[128,512]{1,0:T(8,128)(2,1)S(1)}, u32[]{:S(2)}, u32[]{:S(2)}) collective-permute-start(bf16[128,512]{1,0:T(8,128)(2,1)S(1)} %get-tuple-element.49.mine_ref), channel_id=1, source_target_pairs={{0,1},{1,0},{2,3},{3,2},{4,5},{5,4},{6,7},{7,6},{8,9},{9,8},{10,11... | collective-permute-start | bytes 393224 | tf_op jit(solution)/shard_map/ppermute | solution.py:380
  22.7 3.7 %collective-permute-start.8 = (f32[4,128]{1,0:T(4,128)S(1)}, f32[4,128]{1,0:T(4,128)S(1)}, u32[]{:S(2)}, u32[]{:S(2)}) collective-permute-start(f32[4,128]{1,0:T(4,128)S(1)} %far_score.1.after_ref), channel_id=1, source_target_pairs={{0,4},{2,6},{4,0},{6,2},{8,12},{10,14},{12,8},{14,10},{1,5},{3,7},... | collective-permute-start | bytes 6152 | tf_op jit(solution)/shard_map/ppermute | solution.py:442
  26.3 4.5 %collective-permute-start.9 = (f32[8,128]{1,0:T(8,128)S(1)}, f32[8,128]{1,0:T(8,128)S(1)}, u32[]{:S(2)}, u32[]{:S(2)}) collective-permute-start(f32[8,128]{1,0:T(8,128)S(1)} %pad_maximum_fusion), channel_id=1, source_target_pairs={{0,8},{2,10},{4,12},{6,14},{8,0},{10,2},{12,4},{14,6},{1,9},{3,11}... | collective-permute-start | bytes 12296 | tf_op jit(solution)/shard_map/ppermute | solution.py:442
  30.9 1.2 %collective-permute-start.10 = (f32[24,128]{1,0:T(8,128)S(1)}, f32[24,128]{1,0:T(8,128)S(1)}, u32[]{:S(2)}, u32[]{:S(2)}) collective-permute-start(f32[24,128]{1,0:T(8,128)S(1)} %concatenate.8.near_ref), channel_id=1, source_target_pairs={{0,1},{1,0},{2,3},{3,2},{4,5},{5,4},{6,7},{7,6},{8,9},{9,8},{10,11... | collective-permute-start | bytes 36872 | tf_op jit(solution)/shard_map/ppermute | solution.py:380
